TPU v7x, 32 devices: a whole 2x2x4 slice. The times are simulated.
32 devices in a mesh: row: 4 (over z), col: 8 (over y, x, core).
Axes of the slice: x: 2, y: 2, z: 4, core: 2. Of those that a mesh axis runs over, the one named last changes fastest.
Arguments:
- gradient: float32 [5120, 16384], P('row', 'col'), may hold values from -6 to 6
- eigenbasis: bfloat16 [5120, 5120], P(None, 'row'), may hold values from -0.078125 to 0.078125
- first_moment: float32 [5120, 16384], P('row', 'col'), may hold values from -3 to 3
- second_moment: float32 [5120, 16384], P('row', 'col'), may hold values from 0.05 to 4
Outputs:
- new_first: float32 [5120, 16384], P('row', 'col')
- new_second: float32 [5120, 16384], P('row', 'col')
- direction: float32 [5120, 16384], P('row', 'col')
All inputs are finite; a program needn't handle non-finite values.
Results may differ from a plain program's by a relative error of at most 0.003.
Values may be sent and summed in bfloat16 or wider, within the bound.
A program may use at most 192 MiB of HBM per device.

v0:
```python
import jax
import jax.numpy as jnp
from jax import lax
from jax.sharding import PartitionSpec as P

STEP = 2


def moments(rotated, first_moment, second_moment):
    new_first = 0.9 * first_moment + 0.1 * rotated
    new_second = 0.99 * second_moment + 0.01 * rotated * rotated
    fix_first = 1.0 - 0.9**STEP
    fix_second = 1.0 - 0.99**STEP
    step_low = (new_first / fix_first / (jnp.sqrt(new_second / fix_second) + 1e-08)).astype(
        jnp.bfloat16
    )
    return (new_first, new_second, step_low)


def local(gradient, eigenbasis, first_moment, second_moment):
    grad_low = gradient.astype(jnp.bfloat16)
    grad_whole = lax.all_gather(grad_low, "row", axis=0, tiled=True)
    rotated = lax.dot_general(
        eigenbasis, grad_whole, (((0,), (0,)), ((), ())), preferred_element_type=jnp.float32
    )
    new_first, new_second, step_low = moments(rotated, first_moment, second_moment)
    terms = jnp.dot(eigenbasis, step_low, preferred_element_type=jnp.float32)
    direction = lax.psum_scatter(terms, "row", scatter_dimension=0, tiled=True)
    return (new_first, new_second, direction)


def solution(mesh):
    in_specs = (P("row", "col"), P(None, "row"), P("row", "col"), P("row", "col"))
    out_specs = (P("row", "col"), P("row", "col"), P("row", "col"))
    return jax.shard_map(local, mesh=mesh, in_specs=in_specs, out_specs=out_specs, check_vma=False)
```

profile of v0, /device:TPU:20, one launch (start us, length us, event | category | flops | bytes accessed | tf_op | source)
XLA Modules:
  0.0 1180.4 jit_solution(833712736062818457)
XLA Ops:
  7.2 0.0 all-gather.2.cloned.1.call-start
  7.2 7.2 convert_element_type.6
  14.4 0.0 all-gather.2.cloned.1.call-update
  14.4 0.0 reduce-scatter.2.cloned.1.call-start
  14.4 356.6 %all-gather.2.cloned.1.call-done = bf16[5120,2048]{1,0:T(8,128)(2,1)} async-done(((bf16[1280,2048]{1,0:T(8,128)(2,1)}), bf16[5120,2048]{1,0:T(8,128)(2,1)}) %all-gather.2.cloned.1.call-update) | async-done | bytes 20971536 | tf_op jit(solution)/shard_map/all_gather | solution.py:22
  371.0 41.1 %fusion = (f32[1280,2048]{1,0:T(8,128)}, f32[1280,2048]{1,0:T(8,128)}) fusion(f32[1280,2048]{1,0:T(8,128)} %param.7, f32[1280,2048]{1,0:T(8,128)} %param.6, bf16[5120,1280]{1,0:T(8,128)(2,1)} %param.5, bf16[5120,2048]{1,0:T(8,128)(2,1)} %all-gather.2.cloned.1.call-done), kind=kOutput, calls=%fused_computation.2 | convolution fusion | flops 26861895680 | bytes 76021760 | tf_op jit(solution)/shard_map/dot_general | solution.py:23
  412.1 62.3 %convolution_bitcast_fusion = f32[5120,2048]{0,1:T(8,128)} fusion(bf16[5120,1280]{1,0:T(8,128)(2,1)} %param.5, f32[1280,2048]{1,0:T(8,128)} %get-tuple-element.6, f32[1280,2048]{1,0:T(8,128)} %get-tuple-element.7), kind=kOutput, calls=%fused_computation | convolution fusion | flops 26856652800 | bytes 76021760 | tf_op jit(solution)/shard_map/dot_general | solution.py:27
  474.4 0.0 reduce-scatter.2.cloned.1.call-update
  474.4 687.9 %reduce-scatter.2.cloned.1.call-done = f32[1280,2048]{0,1:T(8,128)} async-done(((f32[5120,2048]{0,1:T(8,128)}), f32[1280,2048]{0,1:T(8,128)}) %reduce-scatter.2.cloned.1.call-update) | async-done | bytes 10485776 | tf_op jit(solution)/shard_map/reduce_scatter | solution.py:28
  1162.4 11.2 copy.7
Async XLA Ops:
  7.2 363.8 %all-gather.2.cloned.1.call-start = ((), (), s32[]{:S(2)}) async-start(), calls=%async_computation.1 | async-start | bytes 26214400 | tf_op jit(solution)/shard_map/all_gather | solution.py:22
  14.4 1148.0 %reduce-scatter.2.cloned.1.call-start = ((), (), s32[]{:S(2)}) async-start(), calls=%async_computation.2 | async-start | bytes 52428800 | tf_op jit(solution)/shard_map/reduce_scatter | solution.py:28
Sparse Core Ops, SparseCore 0:
  14.5 356.4 all-gather.1
  474.6 687.7 reduce-scatter.1
where the time goes:
time: 1180 us
  waiting for transfers between devices  1040 us (88%)
  matrix products  103 us (9%)
  between operations  14 us (1%)
    reduce_scatter x1, waiting for transfers between devices, local(): direction = lax.psum_scatter(terms, 'row', scatter_dimension=0, tiled=True)  688 us
    all_gather x1, waiting for transfers between devices, local(): grad_whole = lax.all_gather(grad_low, 'row', axis=0, tiled=True)  357 us
    dot_general x1, matrix products, local(): terms = jnp.dot(eigenbasis, step_low, preferred_element_type=jnp.float32)  62.3 us
    dot_general x1, matrix products, local(): lax.dot_general(eigenbasis, grad_whole, (((0,), (0,)), ((), ())), preferr...  41.1 us
  transfers between devices with their start and end apart: 2, of which 2 were waited for; matrix products, arithmetic and copies ran while one was open for 0% of the time, Pallas kernels for 0%

commit v1 on v0

v1 whole, which is shorter than its diff:
```python
import jax
import jax.numpy as jnp
from jax import lax
from jax.sharding import PartitionSpec as P

STEP = 2
CHUNKS = 8


def moments(rotated, first_moment, second_moment):
    new_first = 0.9 * first_moment + 0.1 * rotated
    new_second = 0.99 * second_moment + 0.01 * rotated * rotated
    fix_first = 1.0 - 0.9**STEP
    fix_second = 1.0 - 0.99**STEP
    step_low = (new_first / fix_first / (jnp.sqrt(new_second / fix_second) + 1e-08)).astype(
        jnp.bfloat16
    )
    return (new_first, new_second, step_low)


def line_steps(block, terms, n, me):
    whole, total = None, None
    fro, to = [block], [block]
    right, left = 0.0, 0.0
    for s in range(1, n + 1):
        if block is not None and s < n:
            fro.append(lax.ppermute(fro[-1], "row", [(i, i + 1) for i in range(s - 1, n - 1)]))
            to.append(lax.ppermute(to[-1], "row", [(i, i - 1) for i in range(1, n - s + 1)]))
        if terms is not None and s > 1:
            k = s - 1
            ahead = (right + terms[n - k]).astype(jnp.bfloat16)
            behind = (left + terms[k]).astype(jnp.bfloat16)
            if block is not None and k == 1:
                fro[1], to[1], ahead, behind = lax.optimization_barrier((fro[1], to[1], ahead, behind))
            right = lax.ppermute(ahead, "row", [(i, i + 1) for i in range(min(k, n - 1))])
            left = lax.ppermute(behind, "row", [(i, i - 1) for i in range(n - k, n)])
            right, left = right.astype(jnp.float32), left.astype(jnp.float32)
    if block is not None:
        whole = [block] + [jnp.where(me + s < n, to[s], fro[n - s]) for s in range(1, n)]
    if terms is not None:
        total = terms[0] + right + left
    return whole, total


def local(n, gradient, eigenbasis, first_moment, second_moment):
    me = lax.axis_index("row")
    rows, cols = gradient.shape
    chunks = CHUNKS if cols % (CHUNKS * 256) == 0 else 1
    w = cols // chunks
    rolled = jnp.concatenate([eigenbasis, eigenbasis], 0)
    rolled = lax.dynamic_slice_in_dim(rolled, me * rows, n * rows, 0)
    first = second = direction = jnp.zeros((rows, cols), jnp.float32)
    whole, terms = None, None
    for p in range(chunks + 2):
        block = None
        if p < chunks:
            block = gradient[:, p * w : (p + 1) * w]
        block, whole, terms = lax.optimization_barrier((block, whole, terms))
        if block is not None:
            block = block.astype(jnp.bfloat16)
        next_whole, total = line_steps(block, terms, n, me)
        terms = None
        if whole is not None:
            c = (p - 1) * w
            rotated = lax.dot_general(
                rolled, jnp.concatenate(whole, 0), (((0,), (0,)), ((), ())), preferred_element_type=jnp.float32
            )
            new_first, new_second, step_low = moments(
                rotated, first_moment[:, c : c + w], second_moment[:, c : c + w]
            )
            terms = jnp.dot(rolled, step_low, preferred_element_type=jnp.float32)
            terms = [terms[k * rows : (k + 1) * rows] for k in range(n)]
            first = lax.dynamic_update_slice(first, new_first, (0, c))
            second = lax.dynamic_update_slice(second, new_second, (0, c))
        if total is not None:
            direction = lax.dynamic_update_slice(direction, total, (0, (p - 2) * w))
        whole = next_whole
    return first, second, direction


def solution(mesh):
    n = mesh.shape["row"]
    in_specs = (P("row", "col"), P(None, "row"), P("row", "col"), P("row", "col"))
    out_specs = (P("row", "col"), P("row", "col"), P("row", "col"))
    return jax.shard_map(
        lambda *a: local(n, *a), mesh=mesh, in_specs=in_specs, out_specs=out_specs, check_vma=False
    )
```

time: 1180 us -> 671 us (0.57)
  waiting for transfers between devices: 1040 us -> 142 us
  starting transfers between devices: 0.08 us -> 300 us
  other arithmetic: 7.16 us -> 77.3 us
  local copies, waits for them, and re-layouts: 11.2 us -> 29.4 us
    reduce_scatter x1 -> x0, waiting for transfers between devices: 688 us -> none  [local(): direction = lax.psum_scatter(terms, 'row', scatter_dimension=0, tiled=True)]
    all_gather x1 -> x0, waiting for transfers between devices: 357 us -> none  [local(): grad_whole = lax.all_gather(grad_low, 'row', axis=0, tiled=True)]
    ppermute x0 -> x96, starting transfers between devices: none -> 300 us  [the longest x24 129 us: line_steps(): left = lax.ppermute(behind, 'row', [(i, i - 1) for i in range(n - k, n)])]
    ppermute x0 -> x96, waiting for transfers between devices: none -> 142 us  [the longest x24 79.9 us: line_steps(): lax.ppermute(fro[-1], 'row', [(i, i + 1) for i in range(s - 1, n - 1)])]
    select_n x0 -> x24, other arithmetic: none -> 26.4 us  [line_steps(): jnp.where(me + s < n, to[s], fro[n - s])]
    dynamic_update_slice x0 -> x3, local copies, waits for them, and re-layouts: none -> 16.3 us  [the longest x1 5.44 us: local(): direction = lax.dynamic_update_slice(direction, total, (0, (p - 2) * w))]
    concatenate x0 -> x1, other arithmetic: none -> 15.3 us  [local(): rolled = jnp.concatenate([eigenbasis, eigenbasis], 0)]
    dynamic_update_slice x0 -> x7, other arithmetic: none -> 13.8 us  [local(): direction = lax.dynamic_update_slice(direction, total, (0, (p - 2) * w))]
  transfers between devices with their start and end apart: 2 -> 96, of which waited for: 2 -> 22; matrix products, arithmetic and copies ran while one was open for 0% -> 31% of each run, Pallas kernels for 0% -> 0%
where the time goes in v1:
time: 671 us; the launch traced here: 660 us
  starting transfers between devices  300 us (45%)
  waiting for transfers between devices  142 us (21%)
  matrix products  108 us (16%)
  other arithmetic  77.3 us (12%)
  local copies, waits for them, and re-layouts  29.4 us (4%)
    ppermute x24, starting transfers between devices, line_steps(): left = lax.ppermute(behind, 'row', [(i, i - 1) for i in range(n - k, n)])  129 us
    ppermute x24, waiting for transfers between devices, line_steps(): lax.ppermute(fro[-1], 'row', [(i, i + 1) for i in range(s - 1, n - 1)])  79.9 us
    ppermute x24, starting transfers between devices, line_steps(): lax.ppermute(to[-1], 'row', [(i, i - 1) for i in range(1, n - s + 1)])  68.7 us
    ppermute x24, starting transfers between devices, line_steps(): lax.ppermute(fro[-1], 'row', [(i, i + 1) for i in range(s - 1, n - 1)])  66.1 us
    dot_general x8, matrix products, local(): lax.dot_general(rolled, jnp.concatenate(whole, 0), (((0,), (0,)), ((), ()...  61.7 us
    dot_general x8, matrix products, local(): terms = jnp.dot(rolled, step_low, preferred_element_type=jnp.float32)  46.5 us
    ppermute x24, starting transfers between devices, line_steps(): lax.ppermute(ahead, 'row', [(i, i + 1) for i in range(min(k, n - 1))])  35.8 us
    select_n x24, other arithmetic, line_steps(): jnp.where(me + s < n, to[s], fro[n - s])  26.4 us
  transfers between devices with their start and end apart: 96, of which 22 were waited for; matrix products, arithmetic and copies ran while one was open for 31% of the time, Pallas kernels for 0%

profile of v1, /device:TPU:20, one launch (start us, length us, event | category | flops | bytes accessed | tf_op | source)
XLA Modules:
  0.0 659.8 jit_solution(855585864724368628)
XLA Ops:
  0.6 5.9 fusion.186
  12.4 12.5 %collective-permute-done.1 = bf16[1280,256]{1,0:T(8,128)(2,1)S(1)} collective-permute-done((bf16[1280,256]{1,0:T(8,128)(2,1)S(1)}, bf16[1280,256]{1,0:T(8,128)(2,1)S(1)}, u32[]{:S(2)}, u32[]{:S(2)}) %collective-permute-start.1) | collective-permute-done | bytes 655392 | tf_op jit(solution)/shard_map/ppermute | solution.py:27
  32.4 10.2 %collective-permute-done.2 = bf16[1280,256]{1,0:T(8,128)(2,1)} collective-permute-done((bf16[1280,256]{1,0:T(8,128)(2,1)S(1)}, bf16[1280,256]{1,0:T(8,128)(2,1)}, u32[]{:S(2)}, u32[]{:S(2)}) %collective-permute-start.2) | collective-permute-done | bytes 655392 | tf_op jit(solution)/shard_map/ppermute | solution.py:27
  46.8 15.3 %fusion = bf16[5120,1280]{1,0:T(8,128)(2,1)} fusion(s32[]{:T(128)S(6)} %select_n.107, bf16[5120,1280]{1,0:T(8,128)(2,1)} %param.5), kind=kLoop, calls=%fused_computation.2 | loop fusion | flops 26214400 | bytes 26214404 | tf_op jit(solution)/shard_map/concatenate | solution.py:50
  67.6 10.0 %collective-permute-start.6 = (bf16[1280,256]{1,0:T(8,128)(2,1)S(1)}, bf16[1280,256]{1,0:T(8,128)(2,1)S(1)}, u32[]{:S(2)}, u32[]{:S(2)}) collective-permute-start(bf16[1280,256]{1,0:T(8,128)(2,1)S(1)} %get-tuple-element.103), channel_id=1, source_target_pairs={{8,0},{16,8},{24,16},{9,1},{17,9},{25,17},{10,2},{18,10},{26,18},{... | collective-permute-start | bytes 1966088 | tf_op jit(solution)/shard_map/ppermute | solution.py:28
  77.6 9.5 %fusion.65 = (f32[1280,256]{1,0:T(8,128)S(1)}, f32[1280,256]{1,0:T(8,128)S(1)}) fusion(f32[1280,2048]{1,0:T(8,128)} %param.7, f32[1280,2048]{1,0:T(8,128)} %param.6, bf16[5120,1280]{1,0:T(8,128)(2,1)} %fusion, bf16[1280,256]{1,0:T(8,128)(2,1)S(1)} %broadcast_select_fusion.7, bf16[1280,256]{1,0:T(8,128)(2,1)S(1)} %broadcast_select_fusion.15, ...), kind=kOutput, calls=%fused_computation.75 | convolution fusion | flops 3368222720 | bytes 20971520 | tf_op jit(solution)/shard_map/dot_general | solution.py:65
  97.9 5.3 collective-permute-done.8
  106.0 5.4 dynamic_update_slice.72
  111.4 5.4 dynamic_update_slice.80
  117.8 10.7 %collective-permute-start.13 = (bf16[1280,256]{1,0:T(8,128)(2,1)S(1)}, bf16[1280,256]{1,0:T(8,128)(2,1)}, u32[]{:S(2)}, u32[]{:S(2)}) collective-permute-start(bf16[1280,256]{1,0:T(8,128)(2,1)S(1)} %get-tuple-element.112), channel_id=1, source_target_pairs={{8,0},{16,8},{24,16},{9,1},{17,9},{25,17},{10,2},{18,10},{26,18},{... | collective-permute-start | bytes 1966088 | tf_op jit(solution)/shard_map/ppermute | solution.py:28
  130.4 7.2 %fusion.124 = (f32[1280,2048]{1,0:T(8,128)}, f32[1280,2048]{1,0:T(8,128)}, f32[1280,256]{1,0:T(8,128)S(1)}) fusion(f32[1280,2048]{1,0:T(8,128)} %dynamic_update_slice.80, f32[1280,2048]{1,0:T(8,128)} %param.7, f32[1280,2048]{1,0:T(8,128)} %dynamic_update_slice.72, f32[1280,2048]{1,0:T(8,128)} %param.6, bf16[5120,1280]{1,0:T(8,128)(2,1)S(1)} %bitcast.17, ...), kind=kOutput, calls=%fused_computation.208 | convolution fusion | flops 3368222720 | bytes 22282240 | tf_op jit(solution)/shard_map/dot_general | solution.py:65
  137.6 6.0 fusion.74
  152.6 7.1 %collective-permute-done.16 = bf16[1280,256]{1,0:T(8,128)(2,1)S(1)} collective-permute-done((bf16[1280,256]{1,0:T(8,128)(2,1)}, bf16[1280,256]{1,0:T(8,128)(2,1)S(1)}, u32[]{:S(2)}, u32[]{:S(2)}) %collective-permute-start.16) | collective-permute-done | bytes 655392 | tf_op jit(solution)/shard_map/ppermute | solution.py:28
  162.0 10.4 %collective-permute-start.52 = (bf16[1280,256]{1,0:T(8,128)(2,1)S(1)}, bf16[1280,256]{1,0:T(8,128)(2,1)S(1)}, u32[]{:S(2)}, u32[]{:S(2)}) collective-permute-start(bf16[1280,256]{1,0:T(8,128)(2,1)S(1)} %get-tuple-element.248), channel_id=1, source_target_pairs={{16,8},{24,16},{17,9},{25,17},{18,10},{26,18},{19,11},{27,19},{20,... | collective-permute-start | bytes 1966088 | tf_op jit(solution)/shard_map/ppermute | solution.py:36
  176.9 5.4 collective-permute-done.15
  199.1 7.4 %fusion.122 = (f32[1280,2048]{1,0:T(8,128)}, f32[1280,2048]{1,0:T(8,128)}, f32[1280,256]{1,0:T(8,128)S(1)}) fusion(f32[1280,2048]{1,0:T(8,128)} %get-tuple-element.261, f32[1280,2048]{1,0:T(8,128)} %param.7, f32[1280,2048]{1,0:T(8,128)} %get-tuple-element.262, f32[1280,2048]{1,0:T(8,128)} %param.6, bf16[5120,1280]{1,0:T(8,128)(2,1)S(1)} %bitcast.17, ...), kind=kOutput, calls=%fused_computation.207 | convolution fusion | flops 3368222720 | bytes 22282240 | tf_op jit(solution)/shard_map/dot_general | solution.py:65
  206.5 6.0 fusion.75
  225.4 5.4 dynamic_update_slice.88
  234.4 12.2 %collective-permute-start.58 = (bf16[1280,256]{1,0:T(8,128)(2,1)S(1)}, bf16[1280,256]{1,0:T(8,128)(2,1)S(1)}, u32[]{:S(2)}, u32[]{:S(2)}) collective-permute-start(bf16[1280,256]{1,0:T(8,128)(2,1)S(1)} %get-tuple-element.246), channel_id=1, source_target_pairs={{16,8},{24,16},{17,9},{25,17},{18,10},{26,18},{19,11},{27,19},{20,... | collective-permute-start | bytes 1966088 | tf_op jit(solution)/shard_map/ppermute | solution.py:36
  250.2 12.9 %collective-permute-done.21 = bf16[1280,256]{1,0:T(8,128)(2,1)S(1)} collective-permute-done((bf16[1280,256]{1,0:T(8,128)(2,1)S(1)}, bf16[1280,256]{1,0:T(8,128)(2,1)S(1)}, u32[]{:S(2)}, u32[]{:S(2)}) %collective-permute-start.21) | collective-permute-done | bytes 655392 | tf_op jit(solution)/shard_map/ppermute | solution.py:27
  267.1 5.2 collective-permute-start.24
  280.4 7.2 %fusion.120 = (f32[1280,2048]{1,0:T(8,128)}, f32[1280,2048]{1,0:T(8,128)}, f32[1280,256]{1,0:T(8,128)S(1)}) fusion(f32[1280,2048]{1,0:T(8,128)} %get-tuple-element.259, f32[1280,2048]{1,0:T(8,128)} %param.7, f32[1280,2048]{1,0:T(8,128)} %get-tuple-element.260, f32[1280,2048]{1,0:T(8,128)} %param.6, bf16[5120,1280]{1,0:T(8,128)(2,1)S(1)} %bitcast.17, ...), kind=kOutput, calls=%fused_computation.206 | convolution fusion | flops 3368222720 | bytes 22282240 | tf_op jit(solution)/shard_map/dot_general | solution.py:65
  287.6 6.0 fusion.76
  309.7 12.0 %collective-permute-start.64 = (bf16[1280,256]{1,0:T(8,128)(2,1)S(1)}, bf16[1280,256]{1,0:T(8,128)(2,1)S(1)}, u32[]{:S(2)}, u32[]{:S(2)}) collective-permute-start(bf16[1280,256]{1,0:T(8,128)(2,1)S(1)} %get-tuple-element.244), channel_id=1, source_target_pairs={{16,8},{24,16},{17,9},{25,17},{18,10},{26,18},{19,11},{27,19},{20,... | collective-permute-start | bytes 1966088 | tf_op jit(solution)/shard_map/ppermute | solution.py:36
  324.9 8.2 %collective-permute-done.27 = bf16[1280,256]{1,0:T(8,128)(2,1)S(1)} collective-permute-done((bf16[1280,256]{1,0:T(8,128)(2,1)S(1)}, bf16[1280,256]{1,0:T(8,128)(2,1)S(1)}, u32[]{:S(2)}, u32[]{:S(2)}) %collective-permute-start.27) | collective-permute-done | bytes 655392 | tf_op jit(solution)/shard_map/ppermute | solution.py:27
  350.2 7.4 %fusion.118 = (f32[1280,2048]{1,0:T(8,128)}, f32[1280,2048]{1,0:T(8,128)}, f32[1280,256]{1,0:T(8,128)S(1)}) fusion(f32[1280,2048]{1,0:T(8,128)} %get-tuple-element.257, f32[1280,2048]{1,0:T(8,128)} %param.7, f32[1280,2048]{1,0:T(8,128)} %get-tuple-element.258, f32[1280,2048]{1,0:T(8,128)} %param.6, bf16[5120,1280]{1,0:T(8,128)(2,1)S(1)} %bitcast.17, ...), kind=kOutput, calls=%fused_computation.205 | convolution fusion | flops 3368222720 | bytes 22282240 | tf_op jit(solution)/shard_map/dot_general | solution.py:65
  357.6 6.0 fusion.77
  380.3 10.8 %collective-permute-start.70 = (bf16[1280,256]{1,0:T(8,128)(2,1)S(1)}, bf16[1280,256]{1,0:T(8,128)(2,1)S(1)}, u32[]{:S(2)}, u32[]{:S(2)}) collective-permute-start(bf16[1280,256]{1,0:T(8,128)(2,1)S(1)} %get-tuple-element.242), channel_id=1, source_target_pairs={{16,8},{24,16},{17,9},{25,17},{18,10},{26,18},{19,11},{27,19},{20,... | collective-permute-start | bytes 1966088 | tf_op jit(solution)/shard_map/ppermute | solution.py:36
  394.3 7.6 %collective-permute-done.33 = bf16[1280,256]{1,0:T(8,128)(2,1)S(1)} collective-permute-done((bf16[1280,256]{1,0:T(8,128)(2,1)S(1)}, bf16[1280,256]{1,0:T(8,128)(2,1)S(1)}, u32[]{:S(2)}, u32[]{:S(2)}) %collective-permute-start.33) | collective-permute-done | bytes 655392 | tf_op jit(solution)/shard_map/ppermute | solution.py:27
  419.0 7.4 %fusion.116 = (f32[1280,2048]{1,0:T(8,128)}, f32[1280,2048]{1,0:T(8,128)}, f32[1280,256]{1,0:T(8,128)S(1)}) fusion(f32[1280,2048]{1,0:T(8,128)} %get-tuple-element.255, f32[1280,2048]{1,0:T(8,128)} %param.7, f32[1280,2048]{1,0:T(8,128)} %get-tuple-element.256, f32[1280,2048]{1,0:T(8,128)} %param.6, bf16[5120,1280]{1,0:T(8,128)(2,1)S(1)} %bitcast.17, ...), kind=kOutput, calls=%fused_computation.204 | convolution fusion | flops 3368222720 | bytes 22282240 | tf_op jit(solution)/shard_map/dot_general | solution.py:65
  426.4 6.0 fusion.78
  444.0 6.4 collective-permute-done.40
  452.7 10.4 %collective-permute-start.76 = (bf16[1280,256]{1,0:T(8,128)(2,1)S(1)}, bf16[1280,256]{1,0:T(8,128)(2,1)S(1)}, u32[]{:S(2)}, u32[]{:S(2)}) collective-permute-start(bf16[1280,256]{1,0:T(8,128)(2,1)S(1)} %get-tuple-element.240), channel_id=1, source_target_pairs={{16,8},{24,16},{17,9},{25,17},{18,10},{26,18},{19,11},{27,19},{20,... | collective-permute-start | bytes 1966088 | tf_op jit(solution)/shard_map/ppermute | solution.py:36
  465.5 7.3 %collective-permute-done.39 = bf16[1280,256]{1,0:T(8,128)(2,1)S(1)} collective-permute-done((bf16[1280,256]{1,0:T(8,128)(2,1)S(1)}, bf16[1280,256]{1,0:T(8,128)(2,1)S(1)}, u32[]{:S(2)}, u32[]{:S(2)}) %collective-permute-start.39) | collective-permute-done | bytes 655392 | tf_op jit(solution)/shard_map/ppermute | solution.py:27
  485.1 4.8 collective-permute-start.77
  489.9 7.2 %fusion.114 = (f32[1280,2048]{1,0:T(8,128)}, f32[1280,2048]{1,0:T(8,128)}, f32[1280,256]{1,0:T(8,128)S(1)}) fusion(f32[1280,2048]{1,0:T(8,128)} %get-tuple-element.253, f32[1280,2048]{1,0:T(8,128)} %param.7, f32[1280,2048]{1,0:T(8,128)} %get-tuple-element.254, f32[1280,2048]{1,0:T(8,128)} %param.6, bf16[5120,1280]{1,0:T(8,128)(2,1)S(1)} %bitcast.17, ...), kind=kOutput, calls=%fused_computation.203 | convolution fusion | flops 3368222720 | bytes 22282240 | tf_op jit(solution)/shard_map/dot_general | solution.py:65
  497.1 5.8 collective-permute-start.46
  502.9 6.0 fusion.79
  515.4 6.3 collective-permute-done.44
  532.5 8.4 %fusion.113 = (f32[1280,2048]{1,0:T(8,128)}, f32[1280,2048]{1,0:T(8,128)}, f32[1280,256]{1,0:T(8,128)}) fusion(f32[1280,2048]{1,0:T(8,128)} %get-tuple-element.251, f32[1280,2048]{1,0:T(8,128)} %param.7, f32[1280,2048]{1,0:T(8,128)} %get-tuple-element.252, f32[1280,2048]{1,0:T(8,128)} %param.6, bf16[5120,1280]{1,0:T(8,128)(2,1)S(1)} %bitcast.17, ...), kind=kOutput, calls=%fused_computation.202 | convolution fusion | flops 3368222720 | bytes 22282240 | tf_op jit(solution)/shard_map/dot_general | solution.py:65
  541.0 6.4 fusion.80
  557.9 24.5 %collective-permute-start.82 = (bf16[1280,256]{1,0:T(8,128)(2,1)S(1)}, bf16[1280,256]{1,0:T(8,128)(2,1)S(1)}, u32[]{:S(2)}, u32[]{:S(2)}) collective-permute-start(bf16[1280,256]{1,0:T(8,128)(2,1)S(1)} %get-tuple-element.238), channel_id=1, source_target_pairs={{16,8},{24,16},{17,9},{25,17},{18,10},{26,18},{19,11},{27,19},{20,... | collective-permute-start | bytes 1966088 | tf_op jit(solution)/shard_map/ppermute | solution.py:36
  583.9 8.6 %collective-permute-done.91 = bf16[1280,256]{1,0:T(8,128)(2,1)S(1)} collective-permute-done((bf16[1280,256]{1,0:T(8,128)(2,1)S(1)}, bf16[1280,256]{1,0:T(8,128)(2,1)S(1)}, u32[]{:S(2)}, u32[]{:S(2)}) %collective-permute-start.91) | collective-permute-done | bytes 655392 | tf_op jit(solution)/shard_map/ppermute | solution.py:35
  594.1 12.5 %collective-permute-done.79 = bf16[1280,256]{1,0:T(8,128)(2,1)S(1)} collective-permute-done((bf16[1280,256]{1,0:T(8,128)(2,1)S(1)}, bf16[1280,256]{1,0:T(8,128)(2,1)S(1)}, u32[]{:S(2)}, u32[]{:S(2)}) %collective-permute-start.79) | collective-permute-done | bytes 655392 | tf_op jit(solution)/shard_map/ppermute | solution.py:35
  608.9 9.9 %collective-permute-start.88 = (bf16[1280,256]{1,0:T(8,128)(2,1)S(1)}, bf16[1280,256]{1,0:T(8,128)(2,1)S(1)}, u32[]{:S(2)}, u32[]{:S(2)}) collective-permute-start(bf16[1280,256]{1,0:T(8,128)(2,1)S(1)} %add_convert_fusion.5), channel_id=1, source_target_pairs={{16,8},{24,16},{17,9},{25,17},{18,10},{26,18},{19,11},{27,19},{20,... | collective-permute-start | bytes 1966088 | tf_op jit(solution)/shard_map/ppermute | solution.py:36
  632.0 5.3 collective-permute-done.94
  645.5 5.8 collective-permute-done.89
  652.6 5.8 collective-permute-done.95
  (320 shorter events, 261.5 us)
Async XLA Ops:
  28.4 33.7 %collective-permute-start.4 = (bf16[1280,256]{1,0:T(8,128)(2,1)}, bf16[1280,256]{1,0:T(8,128)(2,1)}, u32[]{:S(2)}, u32[]{:S(2)}) collective-permute-start(bf16[1280,256]{1,0:T(8,128)(2,1)} %collective-permute-done), channel_id=1, source_target_pairs={{8,0},{16,8},{9,1},{17,9},{10,2},{18,10},{11,3},{19,11},{12,4},{20... | collective-permute-start | bytes 1966088 | tf_op jit(solution)/shard_map/ppermute | solution.py:28
  65.3 22.5 %collective-permute-start.7 = (bf16[1280,256]{1,0:T(8,128)(2,1)S(1)}, bf16[1280,256]{1,0:T(8,128)(2,1)S(1)}, u32[]{:S(2)}, u32[]{:S(2)}) collective-permute-start(bf16[1280,256]{1,0:T(8,128)(2,1)S(1)} %get-tuple-element.103), channel_id=1, source_target_pairs={{0,8},{8,16},{16,24},{1,9},{9,17},{17,25},{2,10},{10,18},{18,26},{... | collective-permute-start | bytes 1966088 | tf_op jit(solution)/shard_map/ppermute | solution.py:27
  67.6 26.2 %collective-permute-start.6 = (bf16[1280,256]{1,0:T(8,128)(2,1)S(1)}, bf16[1280,256]{1,0:T(8,128)(2,1)S(1)}, u32[]{:S(2)}, u32[]{:S(2)}) collective-permute-start(bf16[1280,256]{1,0:T(8,128)(2,1)S(1)} %get-tuple-element.103), channel_id=1, source_target_pairs={{8,0},{16,8},{24,16},{9,1},{17,9},{25,17},{10,2},{18,10},{26,18},{... | collective-permute-start | bytes 1966088 | tf_op jit(solution)/shard_map/ppermute | solution.py:28
  93.9 22.9 %collective-permute-start.10 = (bf16[1280,256]{1,0:T(8,128)(2,1)S(1)}, bf16[1280,256]{1,0:T(8,128)(2,1)S(1)}, u32[]{:S(2)}, u32[]{:S(2)}) collective-permute-start(bf16[1280,256]{1,0:T(8,128)(2,1)S(1)} %collective-permute-done.6), channel_id=1, source_target_pairs={{8,0},{16,8},{9,1},{17,9},{10,2},{18,10},{11,3},{19,11},{12,4},{20... | collective-permute-start | bytes 1966088 | tf_op jit(solution)/shard_map/ppermute | solution.py:28
  117.8 26.0 %collective-permute-start.13 = (bf16[1280,256]{1,0:T(8,128)(2,1)S(1)}, bf16[1280,256]{1,0:T(8,128)(2,1)}, u32[]{:S(2)}, u32[]{:S(2)}) collective-permute-start(bf16[1280,256]{1,0:T(8,128)(2,1)S(1)} %get-tuple-element.112), channel_id=1, source_target_pairs={{8,0},{16,8},{24,16},{9,1},{17,9},{25,17},{10,2},{18,10},{26,18},{... | collective-permute-start | bytes 1966088 | tf_op jit(solution)/shard_map/ppermute | solution.py:28
  160.7 30.3 %collective-permute-start.49 = (bf16[1280,256]{1,0:T(8,128)(2,1)S(1)}, bf16[1280,256]{1,0:T(8,128)(2,1)S(1)}, u32[]{:S(2)}, u32[]{:S(2)}) collective-permute-start(bf16[1280,256]{1,0:T(8,128)(2,1)S(1)} %get-tuple-element.247), channel_id=1, source_target_pairs={{0,8},{8,16},{1,9},{9,17},{2,10},{10,18},{3,11},{11,19},{4,12},{12... | collective-permute-start | bytes 1966088 | tf_op jit(solution)/shard_map/ppermute | solution.py:35
  162.0 32.1 %collective-permute-start.52 = (bf16[1280,256]{1,0:T(8,128)(2,1)S(1)}, bf16[1280,256]{1,0:T(8,128)(2,1)S(1)}, u32[]{:S(2)}, u32[]{:S(2)}) collective-permute-start(bf16[1280,256]{1,0:T(8,128)(2,1)S(1)} %get-tuple-element.248), channel_id=1, source_target_pairs={{16,8},{24,16},{17,9},{25,17},{18,10},{26,18},{19,11},{27,19},{20,... | collective-permute-start | bytes 1966088 | tf_op jit(solution)/shard_map/ppermute | solution.py:36
  184.3 29.2 %collective-permute-start.19 = (bf16[1280,256]{1,0:T(8,128)(2,1)S(1)}, bf16[1280,256]{1,0:T(8,128)(2,1)}, u32[]{:S(2)}, u32[]{:S(2)}) collective-permute-start(bf16[1280,256]{1,0:T(8,128)(2,1)S(1)} %copy-done.11), channel_id=1, source_target_pairs={{8,0},{16,8},{24,16},{9,1},{17,9},{25,17},{10,2},{18,10},{26,18},{... | collective-permute-start | bytes 1966088 | tf_op jit(solution)/shard_map/ppermute | solution.py:28
  186.3 27.3 %collective-permute-start.18 = (bf16[1280,256]{1,0:T(8,128)(2,1)S(1)}, bf16[1280,256]{1,0:T(8,128)(2,1)}, u32[]{:S(2)}, u32[]{:S(2)}) collective-permute-start(bf16[1280,256]{1,0:T(8,128)(2,1)S(1)} %copy-done.11), channel_id=1, source_target_pairs={{0,8},{8,16},{16,24},{1,9},{9,17},{17,25},{2,10},{10,18},{18,26},{... | collective-permute-start | bytes 1966088 | tf_op jit(solution)/shard_map/ppermute | solution.py:27
  192.0 27.7 %collective-permute-start.50 = (bf16[1280,256]{1,0:T(8,128)(2,1)}, bf16[1280,256]{1,0:T(8,128)(2,1)}, u32[]{:S(2)}, u32[]{:S(2)}) collective-permute-start(bf16[1280,256]{1,0:T(8,128)(2,1)} %add_convert_fusion.30), channel_id=1, source_target_pairs={{0,8},{8,16},{16,24},{1,9},{9,17},{17,25},{2,10},{10,18},{18,26},{... | collective-permute-start | bytes 1966088 | tf_op jit(solution)/shard_map/ppermute | solution.py:35
  195.1 28.8 %collective-permute-start.53 = (bf16[1280,256]{1,0:T(8,128)(2,1)}, bf16[1280,256]{1,0:T(8,128)(2,1)}, u32[]{:S(2)}, u32[]{:S(2)}) collective-permute-start(bf16[1280,256]{1,0:T(8,128)(2,1)} %add_convert_fusion.28), channel_id=1, source_target_pairs={{8,0},{16,8},{24,16},{9,1},{17,9},{25,17},{10,2},{18,10},{26,18},{... | collective-permute-start | bytes 1966088 | tf_op jit(solution)/shard_map/ppermute | solution.py:36
  219.8 26.9 %collective-permute-start.20 = (bf16[1280,256]{1,0:T(8,128)(2,1)}, bf16[1280,256]{1,0:T(8,128)(2,1)S(1)}, u32[]{:S(2)}, u32[]{:S(2)}) collective-permute-start(bf16[1280,256]{1,0:T(8,128)(2,1)} %collective-permute-done.18), channel_id=1, source_target_pairs={{8,16},{16,24},{9,17},{17,25},{10,18},{18,26},{11,19},{19,27},{12,... | collective-permute-start | bytes 1966088 | tf_op jit(solution)/shard_map/ppermute | solution.py:27
  233.1 39.1 %collective-permute-start.55 = (bf16[1280,256]{1,0:T(8,128)(2,1)S(1)}, bf16[1280,256]{1,0:T(8,128)(2,1)S(1)}, u32[]{:S(2)}, u32[]{:S(2)}) collective-permute-start(bf16[1280,256]{1,0:T(8,128)(2,1)S(1)} %get-tuple-element.245), channel_id=1, source_target_pairs={{0,8},{8,16},{1,9},{9,17},{2,10},{10,18},{3,11},{11,19},{4,12},{12... | collective-permute-start | bytes 1966088 | tf_op jit(solution)/shard_map/ppermute | solution.py:35
  234.4 40.9 %collective-permute-start.58 = (bf16[1280,256]{1,0:T(8,128)(2,1)S(1)}, bf16[1280,256]{1,0:T(8,128)(2,1)S(1)}, u32[]{:S(2)}, u32[]{:S(2)}) collective-permute-start(bf16[1280,256]{1,0:T(8,128)(2,1)S(1)} %get-tuple-element.246), channel_id=1, source_target_pairs={{16,8},{24,16},{17,9},{25,17},{18,10},{26,18},{19,11},{27,19},{20,... | collective-permute-start | bytes 1966088 | tf_op jit(solution)/shard_map/ppermute | solution.py:36
  265.1 28.6 %collective-permute-start.25 = (bf16[1280,256]{1,0:T(8,128)(2,1)S(1)}, bf16[1280,256]{1,0:T(8,128)(2,1)}, u32[]{:S(2)}, u32[]{:S(2)}) collective-permute-start(bf16[1280,256]{1,0:T(8,128)(2,1)S(1)} %copy-done.9), channel_id=1, source_target_pairs={{8,0},{16,8},{24,16},{9,1},{17,9},{25,17},{10,2},{18,10},{26,18},{... | collective-permute-start | bytes 1966088 | tf_op jit(solution)/shard_map/ppermute | solution.py:28
  267.1 26.7 %collective-permute-start.24 = (bf16[1280,256]{1,0:T(8,128)(2,1)S(1)}, bf16[1280,256]{1,0:T(8,128)(2,1)S(1)}, u32[]{:S(2)}, u32[]{:S(2)}) collective-permute-start(bf16[1280,256]{1,0:T(8,128)(2,1)S(1)} %copy-done.9), channel_id=1, source_target_pairs={{0,8},{8,16},{16,24},{1,9},{9,17},{17,25},{2,10},{10,18},{18,26},{... | collective-permute-start | bytes 1966088 | tf_op jit(solution)/shard_map/ppermute | solution.py:27
  273.3 25.9 %collective-permute-start.56 = (bf16[1280,256]{1,0:T(8,128)(2,1)}, bf16[1280,256]{1,0:T(8,128)(2,1)}, u32[]{:S(2)}, u32[]{:S(2)}) collective-permute-start(bf16[1280,256]{1,0:T(8,128)(2,1)} %add_convert_fusion.26), channel_id=1, source_target_pairs={{0,8},{8,16},{16,24},{1,9},{9,17},{17,25},{2,10},{10,18},{18,26},{... | collective-permute-start | bytes 1966088 | tf_op jit(solution)/shard_map/ppermute | solution.py:35
  276.5 26.2 %collective-permute-start.59 = (bf16[1280,256]{1,0:T(8,128)(2,1)}, bf16[1280,256]{1,0:T(8,128)(2,1)}, u32[]{:S(2)}, u32[]{:S(2)}) collective-permute-start(bf16[1280,256]{1,0:T(8,128)(2,1)} %add_convert_fusion.24), channel_id=1, source_target_pairs={{8,0},{16,8},{24,16},{9,1},{17,9},{25,17},{10,2},{18,10},{26,18},{... | collective-permute-start | bytes 1966088 | tf_op jit(solution)/shard_map/ppermute | solution.py:36
  308.4 33.5 %collective-permute-start.61 = (bf16[1280,256]{1,0:T(8,128)(2,1)S(1)}, bf16[1280,256]{1,0:T(8,128)(2,1)S(1)}, u32[]{:S(2)}, u32[]{:S(2)}) collective-permute-start(bf16[1280,256]{1,0:T(8,128)(2,1)S(1)} %get-tuple-element.243), channel_id=1, source_target_pairs={{0,8},{8,16},{1,9},{9,17},{2,10},{10,18},{3,11},{11,19},{4,12},{12... | collective-permute-start | bytes 1966088 | tf_op jit(solution)/shard_map/ppermute | solution.py:35
  309.7 35.3 %collective-permute-start.64 = (bf16[1280,256]{1,0:T(8,128)(2,1)S(1)}, bf16[1280,256]{1,0:T(8,128)(2,1)S(1)}, u32[]{:S(2)}, u32[]{:S(2)}) collective-permute-start(bf16[1280,256]{1,0:T(8,128)(2,1)S(1)} %get-tuple-element.244), channel_id=1, source_target_pairs={{16,8},{24,16},{17,9},{25,17},{18,10},{26,18},{19,11},{27,19},{20,... | collective-permute-start | bytes 1966088 | tf_op jit(solution)/shard_map/ppermute | solution.py:36
  335.2 28.6 %collective-permute-start.31 = (bf16[1280,256]{1,0:T(8,128)(2,1)S(1)}, bf16[1280,256]{1,0:T(8,128)(2,1)}, u32[]{:S(2)}, u32[]{:S(2)}) collective-permute-start(bf16[1280,256]{1,0:T(8,128)(2,1)S(1)} %copy-done.7), channel_id=1, source_target_pairs={{8,0},{16,8},{24,16},{9,1},{17,9},{25,17},{10,2},{18,10},{26,18},{... | collective-permute-start | bytes 1966088 | tf_op jit(solution)/shard_map/ppermute | solution.py:28
  337.1 26.7 %collective-permute-start.30 = (bf16[1280,256]{1,0:T(8,128)(2,1)S(1)}, bf16[1280,256]{1,0:T(8,128)(2,1)S(1)}, u32[]{:S(2)}, u32[]{:S(2)}) collective-permute-start(bf16[1280,256]{1,0:T(8,128)(2,1)S(1)} %copy-done.7), channel_id=1, source_target_pairs={{0,8},{8,16},{16,24},{1,9},{9,17},{17,25},{2,10},{10,18},{18,26},{... | collective-permute-start | bytes 1966088 | tf_op jit(solution)/shard_map/ppermute | solution.py:27
  343.0 26.3 %collective-permute-start.62 = (bf16[1280,256]{1,0:T(8,128)(2,1)}, bf16[1280,256]{1,0:T(8,128)(2,1)}, u32[]{:S(2)}, u32[]{:S(2)}) collective-permute-start(bf16[1280,256]{1,0:T(8,128)(2,1)} %add_convert_fusion.22), channel_id=1, source_target_pairs={{0,8},{8,16},{16,24},{1,9},{9,17},{17,25},{2,10},{10,18},{18,26},{... | collective-permute-start | bytes 1966088 | tf_op jit(solution)/shard_map/ppermute | solution.py:35
  346.1 26.6 %collective-permute-start.65 = (bf16[1280,256]{1,0:T(8,128)(2,1)}, bf16[1280,256]{1,0:T(8,128)(2,1)}, u32[]{:S(2)}, u32[]{:S(2)}) collective-permute-start(bf16[1280,256]{1,0:T(8,128)(2,1)} %add_convert_fusion.20), channel_id=1, source_target_pairs={{8,0},{16,8},{24,16},{9,1},{17,9},{25,17},{10,2},{18,10},{26,18},{... | collective-permute-start | bytes 1966088 | tf_op jit(solution)/shard_map/ppermute | solution.py:36
  379.0 31.6 %collective-permute-start.67 = (bf16[1280,256]{1,0:T(8,128)(2,1)S(1)}, bf16[1280,256]{1,0:T(8,128)(2,1)S(1)}, u32[]{:S(2)}, u32[]{:S(2)}) collective-permute-start(bf16[1280,256]{1,0:T(8,128)(2,1)S(1)} %get-tuple-element.241), channel_id=1, source_target_pairs={{0,8},{8,16},{1,9},{9,17},{2,10},{10,18},{3,11},{11,19},{4,12},{12... | collective-permute-start | bytes 1966088 | tf_op jit(solution)/shard_map/ppermute | solution.py:35
  380.3 33.4 %collective-permute-start.70 = (bf16[1280,256]{1,0:T(8,128)(2,1)S(1)}, bf16[1280,256]{1,0:T(8,128)(2,1)S(1)}, u32[]{:S(2)}, u32[]{:S(2)}) collective-permute-start(bf16[1280,256]{1,0:T(8,128)(2,1)S(1)} %get-tuple-element.242), channel_id=1, source_target_pairs={{16,8},{24,16},{17,9},{25,17},{18,10},{26,18},{19,11},{27,19},{20,... | collective-permute-start | bytes 1966088 | tf_op jit(solution)/shard_map/ppermute | solution.py:36
  403.9 28.6 %collective-permute-start.37 = (bf16[1280,256]{1,0:T(8,128)(2,1)S(1)}, bf16[1280,256]{1,0:T(8,128)(2,1)}, u32[]{:S(2)}, u32[]{:S(2)}) collective-permute-start(bf16[1280,256]{1,0:T(8,128)(2,1)S(1)} %copy-done.5), channel_id=1, source_target_pairs={{8,0},{16,8},{24,16},{9,1},{17,9},{25,17},{10,2},{18,10},{26,18},{... | collective-permute-start | bytes 1966088 | tf_op jit(solution)/shard_map/ppermute | solution.py:28
  406.7 25.9 %collective-permute-start.36 = (bf16[1280,256]{1,0:T(8,128)(2,1)S(1)}, bf16[1280,256]{1,0:T(8,128)(2,1)S(1)}, u32[]{:S(2)}, u32[]{:S(2)}) collective-permute-start(bf16[1280,256]{1,0:T(8,128)(2,1)S(1)} %copy-done.5), channel_id=1, source_target_pairs={{0,8},{8,16},{16,24},{1,9},{9,17},{17,25},{2,10},{10,18},{18,26},{... | collective-permute-start | bytes 1966088 | tf_op jit(solution)/shard_map/ppermute | solution.py:27
  411.7 27.6 %collective-permute-start.68 = (bf16[1280,256]{1,0:T(8,128)(2,1)}, bf16[1280,256]{1,0:T(8,128)(2,1)}, u32[]{:S(2)}, u32[]{:S(2)}) collective-permute-start(bf16[1280,256]{1,0:T(8,128)(2,1)} %add_convert_fusion.18), channel_id=1, source_target_pairs={{0,8},{8,16},{16,24},{1,9},{9,17},{17,25},{2,10},{10,18},{18,26},{... | collective-permute-start | bytes 1966088 | tf_op jit(solution)/shard_map/ppermute | solution.py:35
  414.8 26.7 %collective-permute-start.71 = (bf16[1280,256]{1,0:T(8,128)(2,1)}, bf16[1280,256]{1,0:T(8,128)(2,1)}, u32[]{:S(2)}, u32[]{:S(2)}) collective-permute-start(bf16[1280,256]{1,0:T(8,128)(2,1)} %add_convert_fusion.16), channel_id=1, source_target_pairs={{8,0},{16,8},{24,16},{9,1},{17,9},{25,17},{10,2},{18,10},{26,18},{... | collective-permute-start | bytes 1966088 | tf_op jit(solution)/shard_map/ppermute | solution.py:36
  439.3 23.8 %collective-permute-start.38 = (bf16[1280,256]{1,0:T(8,128)(2,1)S(1)}, bf16[1280,256]{1,0:T(8,128)(2,1)S(1)}, u32[]{:S(2)}, u32[]{:S(2)}) collective-permute-start(bf16[1280,256]{1,0:T(8,128)(2,1)S(1)} %copy-done.20), channel_id=1, source_target_pairs={{8,16},{16,24},{9,17},{17,25},{10,18},{18,26},{11,19},{19,27},{12,... | collective-permute-start | bytes 1966088 | tf_op jit(solution)/shard_map/ppermute | solution.py:27
  451.4 29.6 %collective-permute-start.73 = (bf16[1280,256]{1,0:T(8,128)(2,1)S(1)}, bf16[1280,256]{1,0:T(8,128)(2,1)S(1)}, u32[]{:S(2)}, u32[]{:S(2)}) collective-permute-start(bf16[1280,256]{1,0:T(8,128)(2,1)S(1)} %get-tuple-element.239), channel_id=1, source_target_pairs={{0,8},{8,16},{1,9},{9,17},{2,10},{10,18},{3,11},{11,19},{4,12},{12... | collective-permute-start | bytes 1966088 | tf_op jit(solution)/shard_map/ppermute | solution.py:35
  452.7 31.4 %collective-permute-start.76 = (bf16[1280,256]{1,0:T(8,128)(2,1)S(1)}, bf16[1280,256]{1,0:T(8,128)(2,1)S(1)}, u32[]{:S(2)}, u32[]{:S(2)}) collective-permute-start(bf16[1280,256]{1,0:T(8,128)(2,1)S(1)} %get-tuple-element.240), channel_id=1, source_target_pairs={{16,8},{24,16},{17,9},{25,17},{18,10},{26,18},{19,11},{27,19},{20,... | collective-permute-start | bytes 1966088 | tf_op jit(solution)/shard_map/ppermute | solution.py:36
  479.0 29.9 %collective-permute-start.42 = (bf16[1280,256]{1,0:T(8,128)(2,1)S(1)}, bf16[1280,256]{1,0:T(8,128)(2,1)}, u32[]{:S(2)}, u32[]{:S(2)}) collective-permute-start(bf16[1280,256]{1,0:T(8,128)(2,1)S(1)} %copy-done.4), channel_id=1, source_target_pairs={{0,8},{8,16},{16,24},{1,9},{9,17},{17,25},{2,10},{10,18},{18,26},{... | collective-permute-start | bytes 1966088 | tf_op jit(solution)/shard_map/ppermute | solution.py:27
  482.0 66.6 %collective-permute-start.74 = (bf16[1280,256]{1,0:T(8,128)(2,1)}, bf16[1280,256]{1,0:T(8,128)(2,1)}, u32[]{:S(2)}, u32[]{:S(2)}) collective-permute-start(bf16[1280,256]{1,0:T(8,128)(2,1)} %add_convert_fusion.14), channel_id=1, source_target_pairs={{0,8},{8,16},{16,24},{1,9},{9,17},{17,25},{2,10},{10,18},{18,26},{... | collective-permute-start | bytes 1966088 | tf_op jit(solution)/shard_map/ppermute | solution.py:35
  485.1 64.2 %collective-permute-start.77 = (bf16[1280,256]{1,0:T(8,128)(2,1)}, bf16[1280,256]{1,0:T(8,128)(2,1)}, u32[]{:S(2)}, u32[]{:S(2)}) collective-permute-start(bf16[1280,256]{1,0:T(8,128)(2,1)} %add_convert_fusion.12), channel_id=1, source_target_pairs={{8,0},{16,8},{24,16},{9,1},{17,9},{25,17},{10,2},{18,10},{26,18},{... | collective-permute-start | bytes 1966088 | tf_op jit(solution)/shard_map/ppermute | solution.py:36
  513.8 41.2 %collective-permute-start.78 = (bf16[1280,256]{1,0:T(8,128)(2,1)}, bf16[1280,256]{1,0:T(8,128)(2,1)}, u32[]{:S(2)}, u32[]{:S(2)}) collective-permute-start(bf16[1280,256]{1,0:T(8,128)(2,1)} %convert_element_type.360), channel_id=1, source_target_pairs={{0,8},{1,9},{2,10},{3,11},{4,12},{5,13},{6,14},{7,15}} | collective-permute-start | bytes 1966088 | tf_op jit(solution)/shard_map/ppermute | solution.py:35
  524.5 30.5 %collective-permute-start.81 = (bf16[1280,256]{1,0:T(8,128)(2,1)}, bf16[1280,256]{1,0:T(8,128)(2,1)}, u32[]{:S(2)}, u32[]{:S(2)}) collective-permute-start(bf16[1280,256]{1,0:T(8,128)(2,1)} %convert_element_type.361), channel_id=1, source_target_pairs={{24,16},{25,17},{26,18},{27,19},{28,20},{29,21},{30,22},{31,23}} | collective-permute-start | bytes 1966088 | tf_op jit(solution)/shard_map/ppermute | solution.py:36
  552.1 30.3 %collective-permute-start.85 = (bf16[1280,256]{1,0:T(8,128)(2,1)S(1)}, bf16[1280,256]{1,0:T(8,128)(2,1)S(1)}, u32[]{:S(2)}, u32[]{:S(2)}) collective-permute-start(bf16[1280,256]{1,0:T(8,128)(2,1)S(1)} %add_convert_fusion.7), channel_id=1, source_target_pairs={{0,8},{8,16},{1,9},{9,17},{2,10},{10,18},{3,11},{11,19},{4,12},{12... | collective-permute-start | bytes 1966088 | tf_op jit(solution)/shard_map/ppermute | solution.py:35
  553.7 38.9 %collective-permute-start.91 = (bf16[1280,256]{1,0:T(8,128)(2,1)S(1)}, bf16[1280,256]{1,0:T(8,128)(2,1)S(1)}, u32[]{:S(2)}, u32[]{:S(2)}) collective-permute-start(bf16[1280,256]{1,0:T(8,128)(2,1)S(1)} %add_convert_fusion.3), channel_id=1, source_target_pairs={{0,8},{8,16},{1,9},{9,17},{2,10},{10,18},{3,11},{11,19},{4,12},{12... | collective-permute-start | bytes 1966088 | tf_op jit(solution)/shard_map/ppermute | solution.py:35
  556.6 50.0 %collective-permute-start.79 = (bf16[1280,256]{1,0:T(8,128)(2,1)S(1)}, bf16[1280,256]{1,0:T(8,128)(2,1)S(1)}, u32[]{:S(2)}, u32[]{:S(2)}) collective-permute-start(bf16[1280,256]{1,0:T(8,128)(2,1)S(1)} %get-tuple-element.237), channel_id=1, source_target_pairs={{0,8},{8,16},{1,9},{9,17},{2,10},{10,18},{3,11},{11,19},{4,12},{12... | collective-permute-start | bytes 1966088 | tf_op jit(solution)/shard_map/ppermute | solution.py:35
  557.9 63.0 %collective-permute-start.82 = (bf16[1280,256]{1,0:T(8,128)(2,1)S(1)}, bf16[1280,256]{1,0:T(8,128)(2,1)S(1)}, u32[]{:S(2)}, u32[]{:S(2)}) collective-permute-start(bf16[1280,256]{1,0:T(8,128)(2,1)S(1)} %get-tuple-element.238), channel_id=1, source_target_pairs={{16,8},{24,16},{17,9},{25,17},{18,10},{26,18},{19,11},{27,19},{20,... | collective-permute-start | bytes 1966088 | tf_op jit(solution)/shard_map/ppermute | solution.py:36
  582.6 26.1 %collective-permute-start.87 = (bf16[1280,256]{1,0:T(8,128)(2,1)S(1)}, bf16[1280,256]{1,0:T(8,128)(2,1)S(1)}, u32[]{:S(2)}, u32[]{:S(2)}) collective-permute-start(bf16[1280,256]{1,0:T(8,128)(2,1)S(1)} %get-tuple-element.236), channel_id=1, source_target_pairs={{24,16},{25,17},{26,18},{27,19},{28,20},{29,21},{30,22},{31,23}} | collective-permute-start | bytes 1966088 | tf_op jit(solution)/shard_map/ppermute | solution.py:36
  592.8 26.0 %collective-permute-start.93 = (bf16[1280,256]{1,0:T(8,128)(2,1)S(1)}, bf16[1280,256]{1,0:T(8,128)(2,1)S(1)}, u32[]{:S(2)}, u32[]{:S(2)}) collective-permute-start(bf16[1280,256]{1,0:T(8,128)(2,1)S(1)} %get-tuple-element.234), channel_id=1, source_target_pairs={{24,16},{25,17},{26,18},{27,19},{28,20},{29,21},{30,22},{31,23}} | collective-permute-start | bytes 1966088 | tf_op jit(solution)/shard_map/ppermute | solution.py:36
  606.8 32.6 %collective-permute-start.80 = (bf16[1280,256]{1,0:T(8,128)(2,1)S(1)}, bf16[1280,256]{1,0:T(8,128)(2,1)S(1)}, u32[]{:S(2)}, u32[]{:S(2)}) collective-permute-start(bf16[1280,256]{1,0:T(8,128)(2,1)S(1)} %add_convert_fusion.10), channel_id=1, source_target_pairs={{0,8},{8,16},{16,24},{1,9},{9,17},{17,25},{2,10},{10,18},{18,26},{... | collective-permute-start | bytes 1966088 | tf_op jit(solution)/shard_map/ppermute | solution.py:35
  621.1 23.2 %collective-permute-start.83 = (bf16[1280,256]{1,0:T(8,128)(2,1)S(1)}, bf16[1280,256]{1,0:T(8,128)(2,1)S(1)}, u32[]{:S(2)}, u32[]{:S(2)}) collective-permute-start(bf16[1280,256]{1,0:T(8,128)(2,1)S(1)} %add_convert_fusion.8), channel_id=1, source_target_pairs={{8,0},{16,8},{24,16},{9,1},{17,9},{25,17},{10,2},{18,10},{26,18},{... | collective-permute-start | bytes 1966088 | tf_op jit(solution)/shard_map/ppermute | solution.py:36
  623.0 22.5 %collective-permute-start.86 = (bf16[1280,256]{1,0:T(8,128)(2,1)S(1)}, bf16[1280,256]{1,0:T(8,128)(2,1)S(1)}, u32[]{:S(2)}, u32[]{:S(2)}) collective-permute-start(bf16[1280,256]{1,0:T(8,128)(2,1)S(1)} %get-tuple-element.235), channel_id=1, source_target_pairs={{0,8},{8,16},{16,24},{1,9},{9,17},{17,25},{2,10},{10,18},{18,26},{... | collective-permute-start | bytes 1966088 | tf_op jit(solution)/shard_map/ppermute | solution.py:35
  629.9 22.7 %collective-permute-start.92 = (bf16[1280,256]{1,0:T(8,128)(2,1)S(1)}, bf16[1280,256]{1,0:T(8,128)(2,1)S(1)}, u32[]{:S(2)}, u32[]{:S(2)}) collective-permute-start(bf16[1280,256]{1,0:T(8,128)(2,1)S(1)} %get-tuple-element.233), channel_id=1, source_target_pairs={{0,8},{8,16},{16,24},{1,9},{9,17},{17,25},{2,10},{10,18},{18,26},{... | collective-permute-start | bytes 1966088 | tf_op jit(solution)/shard_map/ppermute | solution.py:35
  (85 other events, 1153.6 us)

commit v2 on v1

--- a/solution.py
+++ b/solution.py
@@ -30,8 +30,6 @@
             k = s - 1
             ahead = (right + terms[n - k]).astype(jnp.bfloat16)
             behind = (left + terms[k]).astype(jnp.bfloat16)
-            if block is not None and k == 1:
-                fro[1], to[1], ahead, behind = lax.optimization_barrier((fro[1], to[1], ahead, behind))
             right = lax.ppermute(ahead, "row", [(i, i + 1) for i in range(min(k, n - 1))])
             left = lax.ppermute(behind, "row", [(i, i - 1) for i in range(n - k, n)])
             right, left = right.astype(jnp.float32), left.astype(jnp.float32)
@@ -47,15 +45,19 @@
     rows, cols = gradient.shape
     chunks = CHUNKS if cols % (CHUNKS * 256) == 0 else 1
     w = cols // chunks
-    rolled = jnp.concatenate([eigenbasis, eigenbasis], 0)
-    rolled = lax.dynamic_slice_in_dim(rolled, me * rows, n * rows, 0)
     first = second = direction = jnp.zeros((rows, cols), jnp.float32)
-    whole, terms = None, None
+    older, whole, terms = None, None, None
     for p in range(chunks + 2):
         block = None
         if p < chunks:
             block = gradient[:, p * w : (p + 1) * w]
-        block, whole, terms = lax.optimization_barrier((block, whole, terms))
+        if older is not None and block is not None:
+            block, older, terms = lax.optimization_barrier((block, older, terms))
+        if p == 1:
+            eigenbasis, whole = lax.optimization_barrier((eigenbasis, whole))
+            rolled = lax.dynamic_slice_in_dim(
+                jnp.concatenate([eigenbasis, eigenbasis], 0), me * rows, n * rows, 0
+            )
         if block is not None:
             block = block.astype(jnp.bfloat16)
         next_whole, total = line_steps(block, terms, n, me)
@@ -74,7 +76,7 @@
             second = lax.dynamic_update_slice(second, new_second, (0, c))
         if total is not None:
             direction = lax.dynamic_update_slice(direction, total, (0, (p - 2) * w))
-        whole = next_whole
+        older, whole = whole, next_whole
     return first, second, direction
 
 

time: 671 us -> 716 us (1.067)
  waiting for transfers between devices: 142 us -> 186 us
    ppermute x24, starting transfers between devices: 129 us -> 89.8 us  [line_steps(): left = lax.ppermute(behind, 'row', [(i, i - 1) for i in range(n - k, n)])]
    ppermute x24, waiting for transfers between devices: 22.8 us -> 61.5 us  [line_steps(): left = lax.ppermute(behind, 'row', [(i, i - 1) for i in range(n - k, n)])]
    ppermute x24, starting transfers between devices: 66.1 us -> 91.3 us  [line_steps(): lax.ppermute(fro[-1], 'row', [(i, i + 1) for i in range(s - 1, n - 1)])]
    ppermute x24, waiting for transfers between devices: 21.2 us -> 0.06 us  [line_steps(): lax.ppermute(ahead, 'row', [(i, i + 1) for i in range(min(k, n - 1))])]
    ppermute x24, waiting for transfers between devices: 18.4 us -> 33.8 us  [line_steps(): lax.ppermute(to[-1], 'row', [(i, i - 1) for i in range(1, n - s + 1)])]
    ppermute x24, starting transfers between devices: 68.7 us -> 84 us  [line_steps(): lax.ppermute(to[-1], 'row', [(i, i - 1) for i in range(1, n - s + 1)])]
    select_n x24, other arithmetic: 26.4 us -> 14.5 us  [line_steps(): jnp.where(me + s < n, to[s], fro[n - s])]
    ppermute x24, waiting for transfers between devices: 79.9 us -> 90.2 us  [line_steps(): lax.ppermute(fro[-1], 'row', [(i, i + 1) for i in range(s - 1, n - 1)])]
  transfers between devices with their start and end apart: 96 -> 96, of which waited for: 22 -> 31; matrix products, arithmetic and copies ran while one was open for 31% -> 29% of each run, Pallas kernels for 0% -> 0%
where the time goes in v2:
time: 716 us; the launch traced here: 709 us
  starting transfers between devices  302 us (42%)
  waiting for transfers between devices  186 us (26%)
  matrix products  107 us (15%)
  other arithmetic  78.3 us (11%)
  local copies, waits for them, and re-layouts  33.6 us (5%)
    ppermute x24, starting transfers between devices, line_steps(): lax.ppermute(fro[-1], 'row', [(i, i + 1) for i in range(s - 1, n - 1)])  91.3 us
    ppermute x24, waiting for transfers between devices, line_steps(): lax.ppermute(fro[-1], 'row', [(i, i + 1) for i in range(s - 1, n - 1)])  90.2 us
    ppermute x24, starting transfers between devices, line_steps(): left = lax.ppermute(behind, 'row', [(i, i - 1) for i in range(n - k, n)])  89.8 us
    ppermute x24, starting transfers between devices, line_steps(): lax.ppermute(to[-1], 'row', [(i, i - 1) for i in range(1, n - s + 1)])  84 us
    ppermute x24, waiting for transfers between devices, line_steps(): left = lax.ppermute(behind, 'row', [(i, i - 1) for i in range(n - k, n)])  61.5 us
    dot_general x8, matrix products, local(): lax.dot_general(rolled, jnp.concatenate(whole, 0), (((0,), (0,)), ((), ()...  59.3 us
    dot_general x8, matrix products, local(): terms = jnp.dot(rolled, step_low, preferred_element_type=jnp.float32)  48.2 us
    ppermute x24, starting transfers between devices, line_steps(): lax.ppermute(ahead, 'row', [(i, i + 1) for i in range(min(k, n - 1))])  36.7 us
  transfers between devices with their start and end apart: 96, of which 31 were waited for; matrix products, arithmetic and copies ran while one was open for 29% of the time, Pallas kernels for 0%

profile of v2, /device:TPU:20, one launch (start us, length us, event | category | flops | bytes accessed | tf_op | source)
XLA Modules:
  0.0 709.4 jit_solution(12867050196093675463)
XLA Ops:
  17.7 7.4 %collective-permute-done.1 = bf16[1280,256]{1,0:T(8,128)(2,1)S(1)} collective-permute-done((bf16[1280,256]{1,0:T(8,128)(2,1)S(1)}, bf16[1280,256]{1,0:T(8,128)(2,1)S(1)}, u32[]{:S(2)}, u32[]{:S(2)}) %collective-permute-start.1) | collective-permute-done | bytes 655392 | tf_op jit(solution)/shard_map/ppermute | solution.py:27
  32.6 6.5 collective-permute-done.7
  58.7 7.6 %collective-permute-done.8 = bf16[1280,256]{1,0:T(8,128)(2,1)} collective-permute-done((bf16[1280,256]{1,0:T(8,128)(2,1)S(1)}, bf16[1280,256]{1,0:T(8,128)(2,1)}, u32[]{:S(2)}, u32[]{:S(2)}) %collective-permute-start.8) | collective-permute-done | bytes 655392 | tf_op jit(solution)/shard_map/ppermute | solution.py:27
  73.6 6.8 collective-permute-done.3
  81.7 12.8 %fusion = bf16[5120,1280]{1,0:T(8,128)(2,1)S(1)} fusion(s32[]{:T(128)S(6)} %select_n.113, bf16[5120,1280]{1,0:T(8,128)(2,1)} %param.5), kind=kLoop, calls=%fused_computation.2 | loop fusion | flops 26214400 | bytes 26214404 | tf_op jit(solution)/shard_map/concatenate | solution.py:59
  94.5 5.7 fusion.65
  110.0 5.4 dynamic_update_slice.80
  117.6 7.6 %fusion.128 = (f32[1280,2048]{1,0:T(8,128)}, f32[1280,2048]{1,0:T(8,128)}, f32[1280,256]{1,0:T(8,128)}) fusion(f32[1280,2048]{1,0:T(8,128)} %dynamic_update_slice.80, f32[1280,2048]{1,0:T(8,128)} %param.7, f32[1280,2048]{1,0:T(8,128)} %dynamic_update_slice.72, f32[1280,2048]{1,0:T(8,128)} %param.6, bf16[5120,1280]{1,0:T(8,128)(2,1)S(1)} %fusion, ...), kind=kOutput, calls=%fused_computation.216 | convolution fusion | flops 3368222720 | bytes 22282240 | tf_op jit(solution)/shard_map/dot_general | solution.py:67
  125.2 6.4 fusion.78
  158.9 9.7 %collective-permute-done.19 = bf16[1280,256]{1,0:T(8,128)(2,1)S(1)} collective-permute-done((bf16[1280,256]{1,0:T(8,128)(2,1)S(1)}, bf16[1280,256]{1,0:T(8,128)(2,1)S(1)}, u32[]{:S(2)}, u32[]{:S(2)}) %collective-permute-start.19) | collective-permute-done | bytes 655392 | tf_op jit(solution)/shard_map/ppermute | solution.py:27
  168.5 17.8 %collective-permute-start.16 = (bf16[1280,256]{1,0:T(8,128)(2,1)S(1)}, bf16[1280,256]{1,0:T(8,128)(2,1)S(1)}, u32[]{:S(2)}, u32[]{:S(2)}) collective-permute-start(bf16[1280,256]{1,0:T(8,128)(2,1)S(1)} %collective-permute-done.12), channel_id=1, source_target_pairs={{8,0},{16,8},{9,1},{17,9},{10,2},{18,10},{11,3},{19,11},{12,4},{20... | collective-permute-start | bytes 1966088 | tf_op jit(solution)/shard_map/ppermute | solution.py:28
  188.3 12.1 %collective-permute-start.22 = (bf16[1280,256]{1,0:T(8,128)(2,1)S(1)}, bf16[1280,256]{1,0:T(8,128)(2,1)S(1)}, u32[]{:S(2)}, u32[]{:S(2)}) collective-permute-start(bf16[1280,256]{1,0:T(8,128)(2,1)S(1)} %collective-permute-done.18), channel_id=1, source_target_pairs={{8,0},{16,8},{9,1},{17,9},{10,2},{18,10},{11,3},{19,11},{12,4},{20... | collective-permute-start | bytes 1966088 | tf_op jit(solution)/shard_map/ppermute | solution.py:28
  204.9 5.8 collective-permute-done.14
  212.0 5.4 collective-permute-start.15
  217.5 7.3 %collective-permute-done.20 = bf16[1280,256]{1,0:T(8,128)(2,1)} collective-permute-done((bf16[1280,256]{1,0:T(8,128)(2,1)S(1)}, bf16[1280,256]{1,0:T(8,128)(2,1)}, u32[]{:S(2)}, u32[]{:S(2)}) %collective-permute-start.20) | collective-permute-done | bytes 655392 | tf_op jit(solution)/shard_map/ppermute | solution.py:27
  232.9 6.8 collective-permute-start.21
  239.8 7.2 %fusion.126 = (f32[1280,2048]{1,0:T(8,128)}, f32[1280,2048]{1,0:T(8,128)}, f32[1280,256]{1,0:T(8,128)S(1)}) fusion(f32[1280,2048]{1,0:T(8,128)} %get-tuple-element.141, f32[1280,2048]{1,0:T(8,128)} %param.7, f32[1280,2048]{1,0:T(8,128)} %get-tuple-element.142, f32[1280,2048]{1,0:T(8,128)} %param.6, bf16[5120,1280]{1,0:T(8,128)(2,1)S(1)} %fusion, ...), kind=kOutput, calls=%fused_computation.215 | convolution fusion | flops 3368222720 | bytes 22282240 | tf_op jit(solution)/shard_map/dot_general | solution.py:67
  247.0 6.0 fusion.79
  257.4 6.8 collective-permute-start.52
  272.3 7.8 %fusion.124 = (f32[1280,2048]{1,0:T(8,128)}, f32[1280,2048]{1,0:T(8,128)}, f32[1280,256]{1,0:T(8,128)}) fusion(f32[1280,2048]{1,0:T(8,128)} %get-tuple-element.139, f32[1280,2048]{1,0:T(8,128)} %param.7, f32[1280,2048]{1,0:T(8,128)} %get-tuple-element.140, f32[1280,2048]{1,0:T(8,128)} %param.6, bf16[5120,1280]{1,0:T(8,128)(2,1)S(1)} %fusion, ...), kind=kOutput, calls=%fused_computation.214 | convolution fusion | flops 3368222720 | bytes 22282240 | tf_op jit(solution)/shard_map/dot_general | solution.py:67
  280.1 6.4 fusion.80
  300.3 15.0 %collective-permute-start.59 = (bf16[1280,256]{1,0:T(8,128)(2,1)S(1)}, bf16[1280,256]{1,0:T(8,128)(2,1)S(1)}, u32[]{:S(2)}, u32[]{:S(2)}) collective-permute-start(bf16[1280,256]{1,0:T(8,128)(2,1)S(1)} %add_convert_fusion.24), channel_id=1, source_target_pairs={{8,0},{16,8},{24,16},{9,1},{17,9},{25,17},{10,2},{18,10},{26,18},{... | collective-permute-start | bytes 1966088 | tf_op jit(solution)/shard_map/ppermute | solution.py:34
  326.0 5.4 dynamic_update_slice.88
  335.1 9.5 %collective-permute-done.24 = bf16[1280,256]{1,0:T(8,128)(2,1)S(1)} collective-permute-done((bf16[1280,256]{1,0:T(8,128)(2,1)S(1)}, bf16[1280,256]{1,0:T(8,128)(2,1)S(1)}, u32[]{:S(2)}, u32[]{:S(2)}) %collective-permute-start.24) | collective-permute-done | bytes 655392 | tf_op jit(solution)/shard_map/ppermute | solution.py:28
  350.5 8.1 %collective-permute-done.30 = bf16[1280,256]{1,0:T(8,128)(2,1)S(1)} collective-permute-done((bf16[1280,256]{1,0:T(8,128)(2,1)S(1)}, bf16[1280,256]{1,0:T(8,128)(2,1)S(1)}, u32[]{:S(2)}, u32[]{:S(2)}) %collective-permute-start.30) | collective-permute-done | bytes 655392 | tf_op jit(solution)/shard_map/ppermute | solution.py:28
  370.2 9.0 %collective-permute-done.26 = bf16[1280,256]{1,0:T(8,128)(2,1)S(1)} collective-permute-done((bf16[1280,256]{1,0:T(8,128)(2,1)S(1)}, bf16[1280,256]{1,0:T(8,128)(2,1)S(1)}, u32[]{:S(2)}, u32[]{:S(2)}) %collective-permute-start.26) | collective-permute-done | bytes 655392 | tf_op jit(solution)/shard_map/ppermute | solution.py:27
  380.5 5.4 collective-permute-start.27
  386.0 7.3 %collective-permute-done.32 = bf16[1280,256]{1,0:T(8,128)(2,1)} collective-permute-done((bf16[1280,256]{1,0:T(8,128)(2,1)S(1)}, bf16[1280,256]{1,0:T(8,128)(2,1)}, u32[]{:S(2)}, u32[]{:S(2)}) %collective-permute-start.32) | collective-permute-done | bytes 655392 | tf_op jit(solution)/shard_map/ppermute | solution.py:27
  398.1 5.7 collective-permute-done.27
  405.2 6.4 collective-permute-start.33
  411.7 7.2 %fusion.122 = (f32[1280,2048]{1,0:T(8,128)}, f32[1280,2048]{1,0:T(8,128)}, f32[1280,256]{1,0:T(8,128)S(1)}) fusion(f32[1280,2048]{1,0:T(8,128)} %get-tuple-element.137, f32[1280,2048]{1,0:T(8,128)} %param.7, f32[1280,2048]{1,0:T(8,128)} %get-tuple-element.138, f32[1280,2048]{1,0:T(8,128)} %param.6, bf16[5120,1280]{1,0:T(8,128)(2,1)S(1)} %fusion, ...), kind=kOutput, calls=%fused_computation.213 | convolution fusion | flops 3368222720 | bytes 22282240 | tf_op jit(solution)/shard_map/dot_general | solution.py:67
  418.9 6.0 fusion.81
  440.8 7.8 %fusion.120 = (f32[1280,2048]{1,0:T(8,128)}, f32[1280,2048]{1,0:T(8,128)}, f32[1280,256]{1,0:T(8,128)}) fusion(f32[1280,2048]{1,0:T(8,128)} %get-tuple-element.135, f32[1280,2048]{1,0:T(8,128)} %param.7, f32[1280,2048]{1,0:T(8,128)} %get-tuple-element.136, f32[1280,2048]{1,0:T(8,128)} %param.6, bf16[5120,1280]{1,0:T(8,128)(2,1)S(1)} %fusion, ...), kind=kOutput, calls=%fused_computation.212 | convolution fusion | flops 3368222720 | bytes 22282240 | tf_op jit(solution)/shard_map/dot_general | solution.py:67
  448.6 6.4 fusion.82
  469.0 17.2 %collective-permute-start.71 = (bf16[1280,256]{1,0:T(8,128)(2,1)S(1)}, bf16[1280,256]{1,0:T(8,128)(2,1)S(1)}, u32[]{:S(2)}, u32[]{:S(2)}) collective-permute-start(bf16[1280,256]{1,0:T(8,128)(2,1)S(1)} %add_convert_fusion.16), channel_id=1, source_target_pairs={{8,0},{16,8},{24,16},{9,1},{17,9},{25,17},{10,2},{18,10},{26,18},{... | collective-permute-start | bytes 1966088 | tf_op jit(solution)/shard_map/ppermute | solution.py:34
  504.9 10.4 %collective-permute-done.36 = bf16[1280,256]{1,0:T(8,128)(2,1)S(1)} collective-permute-done((bf16[1280,256]{1,0:T(8,128)(2,1)S(1)}, bf16[1280,256]{1,0:T(8,128)(2,1)S(1)}, u32[]{:S(2)}, u32[]{:S(2)}) %collective-permute-start.36) | collective-permute-done | bytes 655392 | tf_op jit(solution)/shard_map/ppermute | solution.py:28
  527.6 5.6 collective-permute-start.46
  563.8 7.6 %fusion.119 = (f32[1280,2048]{1,0:T(8,128)}, f32[1280,2048]{1,0:T(8,128)}, f32[1280,256]{1,0:T(8,128)}) fusion(f32[1280,2048]{1,0:T(8,128)} %get-tuple-element.133, f32[1280,2048]{1,0:T(8,128)} %param.7, f32[1280,2048]{1,0:T(8,128)} %get-tuple-element.134, f32[1280,2048]{1,0:T(8,128)} %param.6, bf16[5120,1280]{1,0:T(8,128)(2,1)S(1)} %fusion, ...), kind=kOutput, calls=%fused_computation.211 | convolution fusion | flops 3368222720 | bytes 22282240 | tf_op jit(solution)/shard_map/dot_general | solution.py:67
  571.4 6.4 fusion.83
  585.5 8.2 %fusion.117 = (f32[1280,2048]{1,0:T(8,128)}, f32[1280,2048]{1,0:T(8,128)}, f32[1280,256]{1,0:T(8,128)}) fusion(f32[1280,2048]{1,0:T(8,128)} %get-tuple-element.131, f32[1280,2048]{1,0:T(8,128)} %param.7, f32[1280,2048]{1,0:T(8,128)} %get-tuple-element.132, f32[1280,2048]{1,0:T(8,128)} %param.6, bf16[5120,1280]{1,0:T(8,128)(2,1)S(1)} %fusion, ...), kind=kOutput, calls=%fused_computation.210 | convolution fusion | flops 3368222720 | bytes 22282240 | tf_op jit(solution)/shard_map/dot_general | solution.py:67
  593.7 6.4 fusion.84
  612.5 8.1 %collective-permute-done.93 = bf16[1280,256]{1,0:T(8,128)(2,1)S(1)} collective-permute-done((bf16[1280,256]{1,0:T(8,128)(2,1)S(1)}, bf16[1280,256]{1,0:T(8,128)(2,1)S(1)}, u32[]{:S(2)}, u32[]{:S(2)}) %collective-permute-start.93) | collective-permute-done | bytes 655392 | tf_op jit(solution)/shard_map/ppermute | solution.py:34
  620.6 7.8 %collective-permute-start.88 = (bf16[1280,256]{1,0:T(8,128)(2,1)S(1)}, bf16[1280,256]{1,0:T(8,128)(2,1)S(1)}, u32[]{:S(2)}, u32[]{:S(2)}) collective-permute-start(bf16[1280,256]{1,0:T(8,128)(2,1)S(1)} %get-tuple-element.88), channel_id=1, source_target_pairs={{16,8},{24,16},{17,9},{25,17},{18,10},{26,18},{19,11},{27,19},{20,... | collective-permute-start | bytes 1966088 | tf_op jit(solution)/shard_map/ppermute | solution.py:34
  628.7 5.9 collective-permute-done.76
  636.1 12.6 %collective-permute-done.82 = bf16[1280,256]{1,0:T(8,128)(2,1)S(1)} collective-permute-done((bf16[1280,256]{1,0:T(8,128)(2,1)S(1)}, bf16[1280,256]{1,0:T(8,128)(2,1)S(1)}, u32[]{:S(2)}, u32[]{:S(2)}) %collective-permute-start.82) | collective-permute-done | bytes 655392 | tf_op jit(solution)/shard_map/ppermute | solution.py:34
  654.9 7.8 %collective-permute-done.88 = bf16[1280,256]{1,0:T(8,128)(2,1)S(1)} collective-permute-done((bf16[1280,256]{1,0:T(8,128)(2,1)S(1)}, bf16[1280,256]{1,0:T(8,128)(2,1)S(1)}, u32[]{:S(2)}, u32[]{:S(2)}) %collective-permute-start.88) | collective-permute-done | bytes 655392 | tf_op jit(solution)/shard_map/ppermute | solution.py:34
  667.0 9.8 %collective-permute-done.94 = bf16[1280,256]{1,0:T(8,128)(2,1)S(1)} collective-permute-done((bf16[1280,256]{1,0:T(8,128)(2,1)S(1)}, bf16[1280,256]{1,0:T(8,128)(2,1)S(1)}, u32[]{:S(2)}, u32[]{:S(2)}) %collective-permute-start.94) | collective-permute-done | bytes 655392 | tf_op jit(solution)/shard_map/ppermute | solution.py:34
  702.1 5.8 collective-permute-done.95
  (326 shorter events, 322.4 us)
Async XLA Ops:
  66.3 51.1 %collective-permute-start.9 = (bf16[1280,256]{1,0:T(8,128)(2,1)}, bf16[1280,256]{1,0:T(8,128)(2,1)S(1)}, u32[]{:S(2)}, u32[]{:S(2)}) collective-permute-start(bf16[1280,256]{1,0:T(8,128)(2,1)} %collective-permute-done.8), channel_id=1, source_target_pairs={{16,24},{17,25},{18,26},{19,27},{20,28},{21,29},{22,30},{23,31}} | collective-permute-start | bytes 1966088 | tf_op jit(solution)/shard_map/ppermute | solution.py:27
  72.0 45.5 %collective-permute-start.11 = (bf16[1280,256]{1,0:T(8,128)(2,1)}, bf16[1280,256]{1,0:T(8,128)(2,1)}, u32[]{:S(2)}, u32[]{:S(2)}) collective-permute-start(bf16[1280,256]{1,0:T(8,128)(2,1)} %collective-permute-done.10), channel_id=1, source_target_pairs={{8,0},{9,1},{10,2},{11,3},{12,4},{13,5},{14,6},{15,7}} | collective-permute-start | bytes 1966088 | tf_op jit(solution)/shard_map/ppermute | solution.py:28
  143.3 43.0 %collective-permute-start.18 = (bf16[1280,256]{1,0:T(8,128)(2,1)S(1)}, bf16[1280,256]{1,0:T(8,128)(2,1)S(1)}, u32[]{:S(2)}, u32[]{:S(2)}) collective-permute-start(bf16[1280,256]{1,0:T(8,128)(2,1)S(1)} %copy-done.37), channel_id=1, source_target_pairs={{8,0},{16,8},{24,16},{9,1},{17,9},{25,17},{10,2},{18,10},{26,18},{... | collective-permute-start | bytes 1966088 | tf_op jit(solution)/shard_map/ppermute | solution.py:28
  148.1 40.2 %collective-permute-start.49 = (bf16[1280,256]{1,0:T(8,128)(2,1)S(1)}, bf16[1280,256]{1,0:T(8,128)(2,1)S(1)}, u32[]{:S(2)}, u32[]{:S(2)}) collective-permute-start(bf16[1280,256]{1,0:T(8,128)(2,1)S(1)} %add_convert_fusion.31), channel_id=1, source_target_pairs={{0,8},{8,16},{1,9},{9,17},{2,10},{10,18},{3,11},{11,19},{4,12},{12... | collective-permute-start | bytes 1966088 | tf_op jit(solution)/shard_map/ppermute | solution.py:33
  154.5 47.2 %collective-permute-start.55 = (bf16[1280,256]{1,0:T(8,128)(2,1)S(1)}, bf16[1280,256]{1,0:T(8,128)(2,1)S(1)}, u32[]{:S(2)}, u32[]{:S(2)}) collective-permute-start(bf16[1280,256]{1,0:T(8,128)(2,1)S(1)} %add_convert_fusion.27), channel_id=1, source_target_pairs={{0,8},{8,16},{1,9},{9,17},{2,10},{10,18},{3,11},{11,19},{4,12},{12... | collective-permute-start | bytes 1966088 | tf_op jit(solution)/shard_map/ppermute | solution.py:33
  157.0 53.7 %collective-permute-start.14 = (bf16[1280,256]{1,0:T(8,128)(2,1)S(1)}, bf16[1280,256]{1,0:T(8,128)(2,1)S(1)}, u32[]{:S(2)}, u32[]{:S(2)}) collective-permute-start(bf16[1280,256]{1,0:T(8,128)(2,1)S(1)} %collective-permute-done.13), channel_id=1, source_target_pairs={{8,16},{16,24},{9,17},{17,25},{10,18},{18,26},{11,19},{19,27},{12,... | collective-permute-start | bytes 1966088 | tf_op jit(solution)/shard_map/ppermute | solution.py:27
  168.5 43.4 %collective-permute-start.16 = (bf16[1280,256]{1,0:T(8,128)(2,1)S(1)}, bf16[1280,256]{1,0:T(8,128)(2,1)S(1)}, u32[]{:S(2)}, u32[]{:S(2)}) collective-permute-start(bf16[1280,256]{1,0:T(8,128)(2,1)S(1)} %collective-permute-done.12), channel_id=1, source_target_pairs={{8,0},{16,8},{9,1},{17,9},{10,2},{18,10},{11,3},{19,11},{12,4},{20... | collective-permute-start | bytes 1966088 | tf_op jit(solution)/shard_map/ppermute | solution.py:28
  186.4 38.5 %collective-permute-start.20 = (bf16[1280,256]{1,0:T(8,128)(2,1)S(1)}, bf16[1280,256]{1,0:T(8,128)(2,1)}, u32[]{:S(2)}, u32[]{:S(2)}) collective-permute-start(bf16[1280,256]{1,0:T(8,128)(2,1)S(1)} %collective-permute-done.19), channel_id=1, source_target_pairs={{8,16},{16,24},{9,17},{17,25},{10,18},{18,26},{11,19},{19,27},{12,... | collective-permute-start | bytes 1966088 | tf_op jit(solution)/shard_map/ppermute | solution.py:27
  188.3 38.4 %collective-permute-start.22 = (bf16[1280,256]{1,0:T(8,128)(2,1)S(1)}, bf16[1280,256]{1,0:T(8,128)(2,1)S(1)}, u32[]{:S(2)}, u32[]{:S(2)}) collective-permute-start(bf16[1280,256]{1,0:T(8,128)(2,1)S(1)} %collective-permute-done.18), channel_id=1, source_target_pairs={{8,0},{16,8},{9,1},{17,9},{10,2},{18,10},{11,3},{19,11},{12,4},{20... | collective-permute-start | bytes 1966088 | tf_op jit(solution)/shard_map/ppermute | solution.py:28
  201.7 113.9 %collective-permute-start.50 = (bf16[1280,256]{1,0:T(8,128)(2,1)}, bf16[1280,256]{1,0:T(8,128)(2,1)}, u32[]{:S(2)}, u32[]{:S(2)}) collective-permute-start(bf16[1280,256]{1,0:T(8,128)(2,1)} %get-tuple-element.127), channel_id=1, source_target_pairs={{0,8},{8,16},{16,24},{1,9},{9,17},{17,25},{2,10},{10,18},{18,26},{... | collective-permute-start | bytes 1966088 | tf_op jit(solution)/shard_map/ppermute | solution.py:33
  210.7 43.8 %collective-permute-start.51 = (bf16[1280,256]{1,0:T(8,128)(2,1)}, bf16[1280,256]{1,0:T(8,128)(2,1)}, u32[]{:S(2)}, u32[]{:S(2)}) collective-permute-start(bf16[1280,256]{1,0:T(8,128)(2,1)} %get-tuple-element.128), channel_id=1, source_target_pairs={{24,16},{25,17},{26,18},{27,19},{28,20},{29,21},{30,22},{31,23}} | collective-permute-start | bytes 1966088 | tf_op jit(solution)/shard_map/ppermute | solution.py:34
  224.8 92.7 %collective-permute-start.56 = (bf16[1280,256]{1,0:T(8,128)(2,1)}, bf16[1280,256]{1,0:T(8,128)(2,1)}, u32[]{:S(2)}, u32[]{:S(2)}) collective-permute-start(bf16[1280,256]{1,0:T(8,128)(2,1)} %get-tuple-element.125), channel_id=1, source_target_pairs={{0,8},{8,16},{16,24},{1,9},{9,17},{17,25},{2,10},{10,18},{18,26},{... | collective-permute-start | bytes 1966088 | tf_op jit(solution)/shard_map/ppermute | solution.py:33
  231.5 34.6 %collective-permute-start.57 = (bf16[1280,256]{1,0:T(8,128)(2,1)}, bf16[1280,256]{1,0:T(8,128)(2,1)}, u32[]{:S(2)}, u32[]{:S(2)}) collective-permute-start(bf16[1280,256]{1,0:T(8,128)(2,1)} %get-tuple-element.126), channel_id=1, source_target_pairs={{24,16},{25,17},{26,18},{27,19},{28,20},{29,21},{30,22},{31,23}} | collective-permute-start | bytes 1966088 | tf_op jit(solution)/shard_map/ppermute | solution.py:34
  257.4 30.5 %collective-permute-start.52 = (bf16[1280,256]{1,0:T(8,128)(2,1)}, bf16[1280,256]{1,0:T(8,128)(2,1)}, u32[]{:S(2)}, u32[]{:S(2)}) collective-permute-start(bf16[1280,256]{1,0:T(8,128)(2,1)} %add_convert_fusion.29), channel_id=1, source_target_pairs={{16,8},{24,16},{17,9},{25,17},{18,10},{26,18},{19,11},{27,19},{20,... | collective-permute-start | bytes 1966088 | tf_op jit(solution)/shard_map/ppermute | solution.py:34
  266.1 30.9 %collective-permute-start.60 = (bf16[1280,256]{1,0:T(8,128)(2,1)}, bf16[1280,256]{1,0:T(8,128)(2,1)}, u32[]{:S(2)}, u32[]{:S(2)}) collective-permute-start(bf16[1280,256]{1,0:T(8,128)(2,1)} %convert_element_type.368), channel_id=1, source_target_pairs={{0,8},{1,9},{2,10},{3,11},{4,12},{5,13},{6,14},{7,15}} | collective-permute-start | bytes 1966088 | tf_op jit(solution)/shard_map/ppermute | solution.py:33
  289.0 32.5 %collective-permute-start.25 = (bf16[1280,256]{1,0:T(8,128)(2,1)S(1)}, bf16[1280,256]{1,0:T(8,128)(2,1)S(1)}, u32[]{:S(2)}, u32[]{:S(2)}) collective-permute-start(bf16[1280,256]{1,0:T(8,128)(2,1)S(1)} %copy-done.35), channel_id=1, source_target_pairs={{0,8},{8,16},{16,24},{1,9},{9,17},{17,25},{2,10},{10,18},{18,26},{... | collective-permute-start | bytes 1966088 | tf_op jit(solution)/shard_map/ppermute | solution.py:27
  300.3 31.1 %collective-permute-start.59 = (bf16[1280,256]{1,0:T(8,128)(2,1)S(1)}, bf16[1280,256]{1,0:T(8,128)(2,1)S(1)}, u32[]{:S(2)}, u32[]{:S(2)}) collective-permute-start(bf16[1280,256]{1,0:T(8,128)(2,1)S(1)} %add_convert_fusion.24), channel_id=1, source_target_pairs={{8,0},{16,8},{24,16},{9,1},{17,9},{25,17},{10,2},{18,10},{26,18},{... | collective-permute-start | bytes 1966088 | tf_op jit(solution)/shard_map/ppermute | solution.py:34
  315.6 29.0 %collective-permute-start.24 = (bf16[1280,256]{1,0:T(8,128)(2,1)S(1)}, bf16[1280,256]{1,0:T(8,128)(2,1)S(1)}, u32[]{:S(2)}, u32[]{:S(2)}) collective-permute-start(bf16[1280,256]{1,0:T(8,128)(2,1)S(1)} %copy-done.35), channel_id=1, source_target_pairs={{8,0},{16,8},{24,16},{9,1},{17,9},{25,17},{10,2},{18,10},{26,18},{... | collective-permute-start | bytes 1966088 | tf_op jit(solution)/shard_map/ppermute | solution.py:28
  317.5 29.0 %collective-permute-start.31 = (bf16[1280,256]{1,0:T(8,128)(2,1)S(1)}, bf16[1280,256]{1,0:T(8,128)(2,1)S(1)}, u32[]{:S(2)}, u32[]{:S(2)}) collective-permute-start(bf16[1280,256]{1,0:T(8,128)(2,1)S(1)} %copy-done.34), channel_id=1, source_target_pairs={{0,8},{8,16},{16,24},{1,9},{9,17},{17,25},{2,10},{10,18},{18,26},{... | collective-permute-start | bytes 1966088 | tf_op jit(solution)/shard_map/ppermute | solution.py:27
  321.5 37.1 %collective-permute-start.30 = (bf16[1280,256]{1,0:T(8,128)(2,1)S(1)}, bf16[1280,256]{1,0:T(8,128)(2,1)S(1)}, u32[]{:S(2)}, u32[]{:S(2)}) collective-permute-start(bf16[1280,256]{1,0:T(8,128)(2,1)S(1)} %copy-done.34), channel_id=1, source_target_pairs={{8,0},{16,8},{24,16},{9,1},{17,9},{25,17},{10,2},{18,10},{26,18},{... | collective-permute-start | bytes 1966088 | tf_op jit(solution)/shard_map/ppermute | solution.py:28
  323.4 37.1 %collective-permute-start.61 = (bf16[1280,256]{1,0:T(8,128)(2,1)S(1)}, bf16[1280,256]{1,0:T(8,128)(2,1)S(1)}, u32[]{:S(2)}, u32[]{:S(2)}) collective-permute-start(bf16[1280,256]{1,0:T(8,128)(2,1)S(1)} %add_convert_fusion.23), channel_id=1, source_target_pairs={{0,8},{8,16},{1,9},{9,17},{2,10},{10,18},{3,11},{11,19},{4,12},{12... | collective-permute-start | bytes 1966088 | tf_op jit(solution)/shard_map/ppermute | solution.py:33
  331.4 35.5 %collective-permute-start.67 = (bf16[1280,256]{1,0:T(8,128)(2,1)S(1)}, bf16[1280,256]{1,0:T(8,128)(2,1)S(1)}, u32[]{:S(2)}, u32[]{:S(2)}) collective-permute-start(bf16[1280,256]{1,0:T(8,128)(2,1)S(1)} %add_convert_fusion.19), channel_id=1, source_target_pairs={{0,8},{8,16},{1,9},{9,17},{2,10},{10,18},{3,11},{11,19},{4,12},{12... | collective-permute-start | bytes 1966088 | tf_op jit(solution)/shard_map/ppermute | solution.py:33
  344.6 34.6 %collective-permute-start.26 = (bf16[1280,256]{1,0:T(8,128)(2,1)S(1)}, bf16[1280,256]{1,0:T(8,128)(2,1)S(1)}, u32[]{:S(2)}, u32[]{:S(2)}) collective-permute-start(bf16[1280,256]{1,0:T(8,128)(2,1)S(1)} %collective-permute-done.25), channel_id=1, source_target_pairs={{8,16},{16,24},{9,17},{17,25},{10,18},{18,26},{11,19},{19,27},{12,... | collective-permute-start | bytes 1966088 | tf_op jit(solution)/shard_map/ppermute | solution.py:27
  346.5 34.0 %collective-permute-start.28 = (bf16[1280,256]{1,0:T(8,128)(2,1)S(1)}, bf16[1280,256]{1,0:T(8,128)(2,1)S(1)}, u32[]{:S(2)}, u32[]{:S(2)}) collective-permute-start(bf16[1280,256]{1,0:T(8,128)(2,1)S(1)} %collective-permute-done.24), channel_id=1, source_target_pairs={{8,0},{16,8},{9,1},{17,9},{10,2},{18,10},{11,3},{19,11},{12,4},{20... | collective-permute-start | bytes 1966088 | tf_op jit(solution)/shard_map/ppermute | solution.py:28
  358.6 34.7 %collective-permute-start.32 = (bf16[1280,256]{1,0:T(8,128)(2,1)S(1)}, bf16[1280,256]{1,0:T(8,128)(2,1)}, u32[]{:S(2)}, u32[]{:S(2)}) collective-permute-start(bf16[1280,256]{1,0:T(8,128)(2,1)S(1)} %collective-permute-done.31), channel_id=1, source_target_pairs={{8,16},{16,24},{9,17},{17,25},{10,18},{18,26},{11,19},{19,27},{12,... | collective-permute-start | bytes 1966088 | tf_op jit(solution)/shard_map/ppermute | solution.py:27
  360.6 34.7 %collective-permute-start.34 = (bf16[1280,256]{1,0:T(8,128)(2,1)S(1)}, bf16[1280,256]{1,0:T(8,128)(2,1)S(1)}, u32[]{:S(2)}, u32[]{:S(2)}) collective-permute-start(bf16[1280,256]{1,0:T(8,128)(2,1)S(1)} %collective-permute-done.30), channel_id=1, source_target_pairs={{8,0},{16,8},{9,1},{17,9},{10,2},{18,10},{11,3},{19,11},{12,4},{20... | collective-permute-start | bytes 1966088 | tf_op jit(solution)/shard_map/ppermute | solution.py:28
  366.9 119.4 %collective-permute-start.62 = (bf16[1280,256]{1,0:T(8,128)(2,1)}, bf16[1280,256]{1,0:T(8,128)(2,1)}, u32[]{:S(2)}, u32[]{:S(2)}) collective-permute-start(bf16[1280,256]{1,0:T(8,128)(2,1)} %get-tuple-element.123), channel_id=1, source_target_pairs={{0,8},{8,16},{16,24},{1,9},{9,17},{17,25},{2,10},{10,18},{18,26},{... | collective-permute-start | bytes 1966088 | tf_op jit(solution)/shard_map/ppermute | solution.py:33
  379.2 46.1 %collective-permute-start.63 = (bf16[1280,256]{1,0:T(8,128)(2,1)}, bf16[1280,256]{1,0:T(8,128)(2,1)}, u32[]{:S(2)}, u32[]{:S(2)}) collective-permute-start(bf16[1280,256]{1,0:T(8,128)(2,1)} %get-tuple-element.124), channel_id=1, source_target_pairs={{24,16},{25,17},{26,18},{27,19},{28,20},{29,21},{30,22},{31,23}} | collective-permute-start | bytes 1966088 | tf_op jit(solution)/shard_map/ppermute | solution.py:34
  393.4 95.0 %collective-permute-start.68 = (bf16[1280,256]{1,0:T(8,128)(2,1)}, bf16[1280,256]{1,0:T(8,128)(2,1)}, u32[]{:S(2)}, u32[]{:S(2)}) collective-permute-start(bf16[1280,256]{1,0:T(8,128)(2,1)} %get-tuple-element.121), channel_id=1, source_target_pairs={{0,8},{8,16},{16,24},{1,9},{9,17},{17,25},{2,10},{10,18},{18,26},{... | collective-permute-start | bytes 1966088 | tf_op jit(solution)/shard_map/ppermute | solution.py:33
  403.8 30.6 %collective-permute-start.69 = (bf16[1280,256]{1,0:T(8,128)(2,1)}, bf16[1280,256]{1,0:T(8,128)(2,1)}, u32[]{:S(2)}, u32[]{:S(2)}) collective-permute-start(bf16[1280,256]{1,0:T(8,128)(2,1)} %get-tuple-element.122), channel_id=1, source_target_pairs={{24,16},{25,17},{26,18},{27,19},{28,20},{29,21},{30,22},{31,23}} | collective-permute-start | bytes 1966088 | tf_op jit(solution)/shard_map/ppermute | solution.py:34
  434.4 31.3 %collective-permute-start.72 = (bf16[1280,256]{1,0:T(8,128)(2,1)}, bf16[1280,256]{1,0:T(8,128)(2,1)}, u32[]{:S(2)}, u32[]{:S(2)}) collective-permute-start(bf16[1280,256]{1,0:T(8,128)(2,1)} %convert_element_type.392), channel_id=1, source_target_pairs={{0,8},{1,9},{2,10},{3,11},{4,12},{5,13},{6,14},{7,15}} | collective-permute-start | bytes 1966088 | tf_op jit(solution)/shard_map/ppermute | solution.py:33
  457.6 34.7 %collective-permute-start.37 = (bf16[1280,256]{1,0:T(8,128)(2,1)S(1)}, bf16[1280,256]{1,0:T(8,128)(2,1)S(1)}, u32[]{:S(2)}, u32[]{:S(2)}) collective-permute-start(bf16[1280,256]{1,0:T(8,128)(2,1)S(1)} %copy-done.32), channel_id=1, source_target_pairs={{0,8},{8,16},{16,24},{1,9},{9,17},{17,25},{2,10},{10,18},{18,26},{... | collective-permute-start | bytes 1966088 | tf_op jit(solution)/shard_map/ppermute | solution.py:27
  469.0 32.3 %collective-permute-start.71 = (bf16[1280,256]{1,0:T(8,128)(2,1)S(1)}, bf16[1280,256]{1,0:T(8,128)(2,1)S(1)}, u32[]{:S(2)}, u32[]{:S(2)}) collective-permute-start(bf16[1280,256]{1,0:T(8,128)(2,1)S(1)} %add_convert_fusion.16), channel_id=1, source_target_pairs={{8,0},{16,8},{24,16},{9,1},{17,9},{25,17},{10,2},{18,10},{26,18},{... | collective-permute-start | bytes 1966088 | tf_op jit(solution)/shard_map/ppermute | solution.py:34
  486.3 29.0 %collective-permute-start.36 = (bf16[1280,256]{1,0:T(8,128)(2,1)S(1)}, bf16[1280,256]{1,0:T(8,128)(2,1)S(1)}, u32[]{:S(2)}, u32[]{:S(2)}) collective-permute-start(bf16[1280,256]{1,0:T(8,128)(2,1)S(1)} %copy-done.32), channel_id=1, source_target_pairs={{8,0},{16,8},{24,16},{9,1},{17,9},{25,17},{10,2},{18,10},{26,18},{... | collective-permute-start | bytes 1966088 | tf_op jit(solution)/shard_map/ppermute | solution.py:28
  488.4 28.9 %collective-permute-start.43 = (bf16[1280,256]{1,0:T(8,128)(2,1)S(1)}, bf16[1280,256]{1,0:T(8,128)(2,1)S(1)}, u32[]{:S(2)}, u32[]{:S(2)}) collective-permute-start(bf16[1280,256]{1,0:T(8,128)(2,1)S(1)} %copy-done.31), channel_id=1, source_target_pairs={{0,8},{8,16},{16,24},{1,9},{9,17},{17,25},{2,10},{10,18},{18,26},{... | collective-permute-start | bytes 1966088 | tf_op jit(solution)/shard_map/ppermute | solution.py:27
  492.4 33.3 %collective-permute-start.42 = (bf16[1280,256]{1,0:T(8,128)(2,1)S(1)}, bf16[1280,256]{1,0:T(8,128)(2,1)S(1)}, u32[]{:S(2)}, u32[]{:S(2)}) collective-permute-start(bf16[1280,256]{1,0:T(8,128)(2,1)S(1)} %copy-done.31), channel_id=1, source_target_pairs={{8,0},{16,8},{24,16},{9,1},{17,9},{25,17},{10,2},{18,10},{26,18},{... | collective-permute-start | bytes 1966088 | tf_op jit(solution)/shard_map/ppermute | solution.py:28
  494.3 33.3 %collective-permute-start.73 = (bf16[1280,256]{1,0:T(8,128)(2,1)S(1)}, bf16[1280,256]{1,0:T(8,128)(2,1)S(1)}, u32[]{:S(2)}, u32[]{:S(2)}) collective-permute-start(bf16[1280,256]{1,0:T(8,128)(2,1)S(1)} %add_convert_fusion.15), channel_id=1, source_target_pairs={{0,8},{8,16},{1,9},{9,17},{2,10},{10,18},{3,11},{11,19},{4,12},{12... | collective-permute-start | bytes 1966088 | tf_op jit(solution)/shard_map/ppermute | solution.py:33
  501.3 33.2 %collective-permute-start.79 = (bf16[1280,256]{1,0:T(8,128)(2,1)S(1)}, bf16[1280,256]{1,0:T(8,128)(2,1)S(1)}, u32[]{:S(2)}, u32[]{:S(2)}) collective-permute-start(bf16[1280,256]{1,0:T(8,128)(2,1)S(1)} %add_convert_fusion.11), channel_id=1, source_target_pairs={{0,8},{8,16},{1,9},{9,17},{2,10},{10,18},{3,11},{11,19},{4,12},{12... | collective-permute-start | bytes 1966088 | tf_op jit(solution)/shard_map/ppermute | solution.py:33
  534.5 144.7 %collective-permute-start.74 = (bf16[1280,256]{1,0:T(8,128)(2,1)}, bf16[1280,256]{1,0:T(8,128)(2,1)}, u32[]{:S(2)}, u32[]{:S(2)}) collective-permute-start(bf16[1280,256]{1,0:T(8,128)(2,1)} %get-tuple-element.119), channel_id=1, source_target_pairs={{0,8},{8,16},{16,24},{1,9},{9,17},{17,25},{2,10},{10,18},{18,26},{... | collective-permute-start | bytes 1966088 | tf_op jit(solution)/shard_map/ppermute | solution.py:33
  540.3 60.0 %collective-permute-start.75 = (bf16[1280,256]{1,0:T(8,128)(2,1)}, bf16[1280,256]{1,0:T(8,128)(2,1)S(1)}, u32[]{:S(2)}, u32[]{:S(2)}) collective-permute-start(bf16[1280,256]{1,0:T(8,128)(2,1)} %get-tuple-element.120), channel_id=1, source_target_pairs={{24,16},{25,17},{26,18},{27,19},{28,20},{29,21},{30,22},{31,23}} | collective-permute-start | bytes 1966088 | tf_op jit(solution)/shard_map/ppermute | solution.py:34
  547.4 53.8 %collective-permute-start.81 = (bf16[1280,256]{1,0:T(8,128)(2,1)}, bf16[1280,256]{1,0:T(8,128)(2,1)S(1)}, u32[]{:S(2)}, u32[]{:S(2)}) collective-permute-start(bf16[1280,256]{1,0:T(8,128)(2,1)} %get-tuple-element.118), channel_id=1, source_target_pairs={{24,16},{25,17},{26,18},{27,19},{28,20},{29,21},{30,22},{31,23}} | collective-permute-start | bytes 1966088 | tf_op jit(solution)/shard_map/ppermute | solution.py:34
  602.7 31.9 %collective-permute-start.76 = (bf16[1280,256]{1,0:T(8,128)(2,1)S(1)}, bf16[1280,256]{1,0:T(8,128)(2,1)S(1)}, u32[]{:S(2)}, u32[]{:S(2)}) collective-permute-start(bf16[1280,256]{1,0:T(8,128)(2,1)S(1)} %add_convert_fusion.13), channel_id=1, source_target_pairs={{16,8},{24,16},{17,9},{25,17},{18,10},{26,18},{19,11},{27,19},{20,... | collective-permute-start | bytes 1966088 | tf_op jit(solution)/shard_map/ppermute | solution.py:34
  607.2 41.5 %collective-permute-start.82 = (bf16[1280,256]{1,0:T(8,128)(2,1)S(1)}, bf16[1280,256]{1,0:T(8,128)(2,1)S(1)}, u32[]{:S(2)}, u32[]{:S(2)}) collective-permute-start(bf16[1280,256]{1,0:T(8,128)(2,1)S(1)} %add_convert_fusion.9), channel_id=1, source_target_pairs={{16,8},{24,16},{17,9},{25,17},{18,10},{26,18},{19,11},{27,19},{20,... | collective-permute-start | bytes 1966088 | tf_op jit(solution)/shard_map/ppermute | solution.py:34
  611.2 39.7 %collective-permute-start.85 = (bf16[1280,256]{1,0:T(8,128)(2,1)S(1)}, bf16[1280,256]{1,0:T(8,128)(2,1)S(1)}, u32[]{:S(2)}, u32[]{:S(2)}) collective-permute-start(bf16[1280,256]{1,0:T(8,128)(2,1)S(1)} %get-tuple-element.87), channel_id=1, source_target_pairs={{0,8},{8,16},{1,9},{9,17},{2,10},{10,18},{3,11},{11,19},{4,12},{12... | collective-permute-start | bytes 1966088 | tf_op jit(solution)/shard_map/ppermute | solution.py:33
  620.6 42.1 %collective-permute-start.88 = (bf16[1280,256]{1,0:T(8,128)(2,1)S(1)}, bf16[1280,256]{1,0:T(8,128)(2,1)S(1)}, u32[]{:S(2)}, u32[]{:S(2)}) collective-permute-start(bf16[1280,256]{1,0:T(8,128)(2,1)S(1)} %get-tuple-element.88), channel_id=1, source_target_pairs={{16,8},{24,16},{17,9},{25,17},{18,10},{26,18},{19,11},{27,19},{20,... | collective-permute-start | bytes 1966088 | tf_op jit(solution)/shard_map/ppermute | solution.py:34
  634.6 30.4 %collective-permute-start.91 = (bf16[1280,256]{1,0:T(8,128)(2,1)S(1)}, bf16[1280,256]{1,0:T(8,128)(2,1)S(1)}, u32[]{:S(2)}, u32[]{:S(2)}) collective-permute-start(bf16[1280,256]{1,0:T(8,128)(2,1)S(1)} %get-tuple-element.81), channel_id=1, source_target_pairs={{0,8},{8,16},{1,9},{9,17},{2,10},{10,18},{3,11},{11,19},{4,12},{12... | collective-permute-start | bytes 1966088 | tf_op jit(solution)/shard_map/ppermute | solution.py:33
  650.9 40.2 %collective-permute-start.80 = (bf16[1280,256]{1,0:T(8,128)(2,1)S(1)}, bf16[1280,256]{1,0:T(8,128)(2,1)S(1)}, u32[]{:S(2)}, u32[]{:S(2)}) collective-permute-start(bf16[1280,256]{1,0:T(8,128)(2,1)S(1)} %copy-done.30), channel_id=1, source_target_pairs={{0,8},{8,16},{16,24},{1,9},{9,17},{17,25},{2,10},{10,18},{18,26},{... | collective-permute-start | bytes 1966088 | tf_op jit(solution)/shard_map/ppermute | solution.py:33
  665.1 30.0 %collective-permute-start.83 = (bf16[1280,256]{1,0:T(8,128)(2,1)S(1)}, bf16[1280,256]{1,0:T(8,128)(2,1)S(1)}, u32[]{:S(2)}, u32[]{:S(2)}) collective-permute-start(bf16[1280,256]{1,0:T(8,128)(2,1)S(1)} %add_convert_fusion.8), channel_id=1, source_target_pairs={{8,0},{16,8},{24,16},{9,1},{17,9},{25,17},{10,2},{18,10},{26,18},{... | collective-permute-start | bytes 1966088 | tf_op jit(solution)/shard_map/ppermute | solution.py:34
  (90 other events, 1432.4 us)

commit v3 on v1

v3 whole, which is shorter than its diff:
```python
import jax
import jax.numpy as jnp
from jax import lax
from jax.sharding import PartitionSpec as P

STEP = 2
CHUNKS = 8


def moments(rotated, first_moment, second_moment):
    new_first = 0.9 * first_moment + 0.1 * rotated
    new_second = 0.99 * second_moment + 0.01 * rotated * rotated
    fix_first = 1.0 - 0.9**STEP
    fix_second = 1.0 - 0.99**STEP
    step_low = (new_first / fix_first / (jnp.sqrt(new_second / fix_second) + 1e-08)).astype(
        jnp.bfloat16
    )
    return (new_first, new_second, step_low)


def line_steps(block, terms, upcoming, prior, n, me):
    whole = None
    fro, to = [block], [block]
    right, left = 0.0, 0.0
    for s in range(1, n + 1):
        ahead, behind = None, None
        if terms is not None and s > 1:
            ahead = (right + terms[n - s + 1]).astype(jnp.bfloat16)
            behind = (left + terms[s - 1]).astype(jnp.bfloat16)
        if s == 2:
            fro[-1], to[-1], ahead, behind, prior = lax.optimization_barrier((fro[-1], to[-1], ahead, behind, prior))
        elif s == n and block is not None:
            fro[-1], to[-1], ahead, behind, upcoming = lax.optimization_barrier(
                (fro[-1], to[-1], ahead, behind, upcoming)
            )
        elif s > 2:
            fro[-1], to[-1], ahead, behind = lax.optimization_barrier((fro[-1], to[-1], ahead, behind))
        if block is not None and s < n:
            fro.append(lax.ppermute(fro[-1], "row", [(i, i + 1) for i in range(s - 1, n - 1)]))
            to.append(lax.ppermute(to[-1], "row", [(i, i - 1) for i in range(1, n - s + 1)]))
        if ahead is not None:
            k = s - 1
            right = lax.ppermute(ahead, "row", [(i, i + 1) for i in range(k)])
            left = lax.ppermute(behind, "row", [(i, i - 1) for i in range(n - k, n)])
    if block is not None:
        whole = [block] + [jnp.where(me + s < n, to[s], fro[n - s]) for s in range(1, n)]
    arrived = None if terms is None else (right, left)
    return whole, arrived, upcoming, prior


def local(n, gradient, eigenbasis, first_moment, second_moment):
    me = lax.axis_index("row")
    rows, cols = gradient.shape
    chunks = CHUNKS if cols % (CHUNKS * 256) == 0 else 1
    w = cols // chunks
    rolled = jnp.concatenate([eigenbasis, eigenbasis], 0)
    rolled = lax.dynamic_slice_in_dim(rolled, me * rows, n * rows, 0)
    first, second, direction = (jnp.full((rows, cols), v, jnp.float32) for v in (0.0, 1.0, 2.0))
    whole, prior, own = None, None, None
    blocks = [gradient[:, c * w : (c + 1) * w].astype(jnp.bfloat16) for c in range(chunks)] + [None]
    block = blocks[0]
    for p in range(chunks + 1):
        terms = None
        if whole is not None:
            c = (p - 1) * w
            rotated = lax.dot_general(
                rolled, jnp.concatenate(whole, 0), (((0,), (0,)), ((), ())), preferred_element_type=jnp.float32
            )
            new_first, new_second, step_low = moments(
                rotated, first_moment[:, c : c + w], second_moment[:, c : c + w]
            )
            terms = jnp.dot(rolled, step_low, preferred_element_type=jnp.float32)
            terms = [terms[k * rows : (k + 1) * rows] for k in range(n)]
            first = lax.dynamic_update_slice(first, new_first, (0, c))
            second = lax.dynamic_update_slice(second, new_second, (0, c))
        upcoming = blocks[p + 1] if p < chunks else None
        whole, arrived, block, prior = line_steps(block, terms, upcoming, prior, n, me)
        if prior is not None:
            direction = lax.dynamic_update_slice(direction, own + prior[0] + prior[1], (0, (p - 2) * w))
        prior, own = arrived, None if terms is None else terms[0]
    direction = lax.dynamic_update_slice(direction, own + prior[0] + prior[1], (0, (chunks - 1) * w))
    return first, second, direction


def solution(mesh):
    n = mesh.shape["row"]
    in_specs = (P("row", "col"), P(None, "row"), P("row", "col"), P("row", "col"))
    out_specs = (P("row", "col"), P("row", "col"), P("row", "col"))
    return jax.shard_map(
        lambda *a: local(n, *a), mesh=mesh, in_specs=in_specs, out_specs=out_specs, check_vma=False
    )
```

time: 671 us -> 676 us (level)
  starting transfers between devices: 300 us -> 233 us
  waiting for transfers between devices: 142 us -> 209 us
  local copies, waits for them, and re-layouts: 29.4 us -> 15.3 us
  matrix products: 108 us -> 118 us
  other arithmetic: 77.3 us -> 85.8 us
    ppermute x24, waiting for transfers between devices: 22.8 us -> 95.8 us  [line_steps(): left = lax.ppermute(behind, 'row', [(i, i - 1) for i in range(n - k, n)])]
    ppermute x24, waiting for transfers between devices: 79.9 us -> 34.5 us  [line_steps(): lax.ppermute(fro[-1], 'row', [(i, i + 1) for i in range(s - 1, n - 1)])]
    ppermute x24, starting transfers between devices: 129 us -> 84.5 us  [line_steps(): left = lax.ppermute(behind, 'row', [(i, i - 1) for i in range(n - k, n)])]
    ppermute x24, waiting for transfers between devices: 21.2 us -> 52.2 us  [line_steps(): right = lax.ppermute(ahead, 'row', [(i, i + 1) for i in range(k)])]
    ppermute x24, starting transfers between devices: 68.7 us -> 54.7 us  [line_steps(): lax.ppermute(to[-1], 'row', [(i, i - 1) for i in range(1, n - s + 1)])]
    select_n x24 -> x23, other arithmetic: 26.4 us -> 35.3 us  [line_steps(): jnp.where(me + s < n, to[s], fro[n - s])]
    ppermute x24, waiting for transfers between devices: 18.4 us -> 26.1 us  [line_steps(): lax.ppermute(to[-1], 'row', [(i, i - 1) for i in range(1, n - s + 1)])]
    convert_element_type x40 -> x16, other arithmetic: 20.3 us -> 16.9 us  [line_steps(): behind = (left + terms[s - 1]).astype(jnp.bfloat16)]
  transfers between devices with their start and end apart: 96 -> 96, of which waited for: 22 -> 41; matrix products, arithmetic and copies ran while one was open for 31% -> 31% of each run, Pallas kernels for 0% -> 0%
where the time goes in v3:
time: 676 us; the launch traced here: 664 us
  starting transfers between devices  233 us (34%)
  waiting for transfers between devices  209 us (31%)
  matrix products  118 us (17%)
  other arithmetic  85.8 us (13%)
  local copies, waits for them, and re-layouts  15.3 us (2%)
    ppermute x24, waiting for transfers between devices, line_steps(): left = lax.ppermute(behind, 'row', [(i, i - 1) for i in range(n - k, n)])  95.8 us
    ppermute x24, starting transfers between devices, line_steps(): left = lax.ppermute(behind, 'row', [(i, i - 1) for i in range(n - k, n)])  84.5 us
    dot_general x8, matrix products, local(): lax.dot_general(rolled, jnp.concatenate(whole, 0), (((0,), (0,)), ((), ()...  66.1 us
    ppermute x24, starting transfers between devices, line_steps(): lax.ppermute(fro[-1], 'row', [(i, i + 1) for i in range(s - 1, n - 1)])  62.6 us
    ppermute x24, starting transfers between devices, line_steps(): lax.ppermute(to[-1], 'row', [(i, i - 1) for i in range(1, n - s + 1)])  54.7 us
    ppermute x24, waiting for transfers between devices, line_steps(): right = lax.ppermute(ahead, 'row', [(i, i + 1) for i in range(k)])  52.2 us
    dot_general x8, matrix products, local(): terms = jnp.dot(rolled, step_low, preferred_element_type=jnp.float32)  52 us
    select_n x23, other arithmetic, line_steps(): jnp.where(me + s < n, to[s], fro[n - s])  35.3 us
  transfers between devices with their start and end apart: 96, of which 41 were waited for; matrix products, arithmetic and copies ran while one was open for 31% of the time, Pallas kernels for 0%

profile of v3, /device:TPU:20, one launch (start us, length us, event | category | flops | bytes accessed | tf_op | source)
XLA Modules:
  0.0 663.7 jit_solution(17794768031336141548)
XLA Ops:
  0.6 4.8 convert.10
  13.3 12.5 %collective-permute-done.1 = bf16[1280,256]{1,0:T(8,128)(2,1)S(1)} collective-permute-done((bf16[1280,256]{1,0:T(8,128)(2,1)S(1)}, bf16[1280,256]{1,0:T(8,128)(2,1)S(1)}, u32[]{:S(2)}, u32[]{:S(2)}) %collective-permute-start.1) | collective-permute-done | bytes 655392 | tf_op jit(solution)/shard_map/ppermute | solution.py:40
  32.3 10.8 %collective-permute-done.3 = bf16[1280,256]{1,0:T(8,128)(2,1)S(1)} collective-permute-done((bf16[1280,256]{1,0:T(8,128)(2,1)S(1)}, bf16[1280,256]{1,0:T(8,128)(2,1)S(1)}, u32[]{:S(2)}, u32[]{:S(2)}) %collective-permute-start.3) | collective-permute-done | bytes 655392 | tf_op jit(solution)/shard_map/ppermute | solution.py:40
  52.0 15.3 %fusion = bf16[5120,1280]{1,0:T(8,128)(2,1)} fusion(s32[]{:T(128)S(6)} %select_n.107, bf16[5120,1280]{1,0:T(8,128)(2,1)} %param.5), kind=kLoop, calls=%fused_computation.2 | loop fusion | flops 26214400 | bytes 26214404 | tf_op jit(solution)/shard_map/concatenate | solution.py:56
  74.9 9.5 %fusion.65 = (f32[1280,256]{1,0:T(8,128)S(1)}, f32[1280,256]{1,0:T(8,128)S(1)}) fusion(f32[1280,2048]{1,0:T(8,128)} %param.7, f32[1280,2048]{1,0:T(8,128)} %param.6, bf16[5120,1280]{1,0:T(8,128)(2,1)} %fusion, bf16[1280,256]{1,0:T(8,128)(2,1)S(1)} %get-tuple-element.316, bf16[1280,256]{1,0:T(8,128)(2,1)S(1)} %broadcast_select_fusion.15, ...), kind=kOutput, calls=%fused_computation.75 | convolution fusion | flops 3368222720 | bytes 20971520 | tf_op jit(solution)/shard_map/dot_general | solution.py:66
  96.4 8.8 %collective-permute-done.11 = bf16[1280,256]{1,0:T(8,128)(2,1)S(1)} collective-permute-done((bf16[1280,256]{1,0:T(8,128)(2,1)S(1)}, bf16[1280,256]{1,0:T(8,128)(2,1)S(1)}, u32[]{:S(2)}, u32[]{:S(2)}) %collective-permute-start.11) | collective-permute-done | bytes 655392 | tf_op jit(solution)/shard_map/ppermute | solution.py:44
  109.7 4.6 collective-permute-start.15
  115.7 5.4 dynamic_update_slice.80
  127.7 5.4 collective-permute-done.12
  135.1 4.6 collective-permute-start.16
  147.8 8.0 %fusion.139 = (f32[1280,2048]{1,0:T(8,128)}, f32[1280,2048]{1,0:T(8,128)S(1)}, f32[1280,256]{1,0:T(8,128)}) fusion(f32[1280,2048]{1,0:T(8,128)} %dynamic_update_slice.80, f32[1280,2048]{1,0:T(8,128)} %param.7, f32[1280,2048]{1,0:T(8,128)S(1)} %dynamic_update_slice.72, f32[1280,2048]{1,0:T(8,128)} %param.6, bf16[5120,1280]{1,0:T(8,128)(2,1)S(1)} %bitcast.17, ...), kind=kOutput, calls=%fused_computation.239 | convolution fusion | flops 3368222720 | bytes 22282240 | tf_op jit(solution)/shard_map/dot_general | solution.py:66
  155.8 6.4 fusion.89
  164.8 5.9 collective-permute-start.21
  179.2 10.0 %collective-permute-done.20 = bf16[1280,256]{1,0:T(8,128)(2,1)S(1)} collective-permute-done((bf16[1280,256]{1,0:T(8,128)(2,1)}, bf16[1280,256]{1,0:T(8,128)(2,1)S(1)}, u32[]{:S(2)}, u32[]{:S(2)}) %collective-permute-start.20) | collective-permute-done | bytes 655392 | tf_op jit(solution)/shard_map/ppermute | solution.py:39
  190.5 4.6 collective-permute-start.27
  198.1 6.8 %collective-permute-done.26 = bf16[1280,256]{1,0:T(8,128)(2,1)S(1)} collective-permute-done((bf16[1280,256]{1,0:T(8,128)(2,1)S(1)}, bf16[1280,256]{1,0:T(8,128)(2,1)S(1)}, u32[]{:S(2)}, u32[]{:S(2)}) %collective-permute-start.26) | collective-permute-done | bytes 655392 | tf_op jit(solution)/shard_map/ppermute | solution.py:43
  205.0 4.7 collective-permute-done.27
  228.0 8.1 %fusion.137 = (f32[1280,2048]{1,0:T(8,128)}, f32[1280,2048]{1,0:T(8,128)S(1)}, f32[1280,256]{1,0:T(8,128)}) fusion(f32[1280,2048]{1,0:T(8,128)} %get-tuple-element.305, f32[1280,2048]{1,0:T(8,128)} %param.7, f32[1280,2048]{1,0:T(8,128)S(1)} %get-tuple-element.306, f32[1280,2048]{1,0:T(8,128)} %param.6, bf16[5120,1280]{1,0:T(8,128)(2,1)S(1)} %bitcast.17, ...), kind=kOutput, calls=%fused_computation.238 | convolution fusion | flops 3368222720 | bytes 22282240 | tf_op jit(solution)/shard_map/dot_general | solution.py:66
  236.1 6.5 fusion.90
  250.1 11.4 %collective-permute-done.35 = bf16[1280,256]{1,0:T(8,128)(2,1)S(1)} collective-permute-done((bf16[1280,256]{1,0:T(8,128)(2,1)S(1)}, bf16[1280,256]{1,0:T(8,128)(2,1)S(1)}, u32[]{:S(2)}, u32[]{:S(2)}) %collective-permute-start.35) | collective-permute-done | bytes 655392 | tf_op jit(solution)/shard_map/ppermute | solution.py:44
  264.1 4.6 collective-permute-start.39
  271.7 9.1 %collective-permute-done.38 = bf16[1280,256]{1,0:T(8,128)(2,1)S(1)} collective-permute-done((bf16[1280,256]{1,0:T(8,128)(2,1)S(1)}, bf16[1280,256]{1,0:T(8,128)(2,1)S(1)}, u32[]{:S(2)}, u32[]{:S(2)}) %collective-permute-start.38) | collective-permute-done | bytes 655392 | tf_op jit(solution)/shard_map/ppermute | solution.py:43
  302.1 8.0 %fusion.135 = (f32[1280,2048]{1,0:T(8,128)}, f32[1280,2048]{1,0:T(8,128)S(1)}, f32[1280,256]{1,0:T(8,128)}) fusion(f32[1280,2048]{1,0:T(8,128)} %get-tuple-element.303, f32[1280,2048]{1,0:T(8,128)} %param.7, f32[1280,2048]{1,0:T(8,128)S(1)} %get-tuple-element.304, f32[1280,2048]{1,0:T(8,128)} %param.6, bf16[5120,1280]{1,0:T(8,128)(2,1)S(1)} %bitcast.17, ...), kind=kOutput, calls=%fused_computation.237 | convolution fusion | flops 3368222720 | bytes 22282240 | tf_op jit(solution)/shard_map/dot_general | solution.py:66
  310.1 6.4 fusion.91
  324.0 11.3 %collective-permute-done.47 = bf16[1280,256]{1,0:T(8,128)(2,1)S(1)} collective-permute-done((bf16[1280,256]{1,0:T(8,128)(2,1)S(1)}, bf16[1280,256]{1,0:T(8,128)(2,1)S(1)}, u32[]{:S(2)}, u32[]{:S(2)}) %collective-permute-start.47) | collective-permute-done | bytes 655392 | tf_op jit(solution)/shard_map/ppermute | solution.py:44
  338.0 4.6 collective-permute-start.51
  345.5 8.1 %collective-permute-done.50 = bf16[1280,256]{1,0:T(8,128)(2,1)S(1)} collective-permute-done((bf16[1280,256]{1,0:T(8,128)(2,1)S(1)}, bf16[1280,256]{1,0:T(8,128)(2,1)S(1)}, u32[]{:S(2)}, u32[]{:S(2)}) %collective-permute-start.50) | collective-permute-done | bytes 655392 | tf_op jit(solution)/shard_map/ppermute | solution.py:43
  376.1 8.0 %fusion.133 = (f32[1280,2048]{1,0:T(8,128)}, f32[1280,2048]{1,0:T(8,128)S(1)}, f32[1280,256]{1,0:T(8,128)}) fusion(f32[1280,2048]{1,0:T(8,128)} %get-tuple-element.301, f32[1280,2048]{1,0:T(8,128)} %param.7, f32[1280,2048]{1,0:T(8,128)S(1)} %get-tuple-element.302, f32[1280,2048]{1,0:T(8,128)} %param.6, bf16[5120,1280]{1,0:T(8,128)(2,1)S(1)} %bitcast.17, ...), kind=kOutput, calls=%fused_computation.236 | convolution fusion | flops 3368222720 | bytes 22282240 | tf_op jit(solution)/shard_map/dot_general | solution.py:66
  384.1 6.4 fusion.92
  398.6 10.8 %collective-permute-done.59 = bf16[1280,256]{1,0:T(8,128)(2,1)S(1)} collective-permute-done((bf16[1280,256]{1,0:T(8,128)(2,1)S(1)}, bf16[1280,256]{1,0:T(8,128)(2,1)S(1)}, u32[]{:S(2)}, u32[]{:S(2)}) %collective-permute-start.59) | collective-permute-done | bytes 655392 | tf_op jit(solution)/shard_map/ppermute | solution.py:44
  412.0 4.6 collective-permute-start.63
  419.6 9.8 %collective-permute-done.62 = bf16[1280,256]{1,0:T(8,128)(2,1)S(1)} collective-permute-done((bf16[1280,256]{1,0:T(8,128)(2,1)S(1)}, bf16[1280,256]{1,0:T(8,128)(2,1)S(1)}, u32[]{:S(2)}, u32[]{:S(2)}) %collective-permute-start.62) | collective-permute-done | bytes 655392 | tf_op jit(solution)/shard_map/ppermute | solution.py:43
  435.0 4.8 collective-permute-start.64
  449.8 8.0 %fusion.131 = (f32[1280,2048]{1,0:T(8,128)}, f32[1280,2048]{1,0:T(8,128)S(1)}, f32[1280,256]{1,0:T(8,128)}) fusion(f32[1280,2048]{1,0:T(8,128)} %get-tuple-element.299, f32[1280,2048]{1,0:T(8,128)} %param.7, f32[1280,2048]{1,0:T(8,128)S(1)} %get-tuple-element.300, f32[1280,2048]{1,0:T(8,128)} %param.6, bf16[5120,1280]{1,0:T(8,128)(2,1)S(1)} %bitcast.17, ...), kind=kOutput, calls=%fused_computation.235 | convolution fusion | flops 3368222720 | bytes 22282240 | tf_op jit(solution)/shard_map/dot_general | solution.py:66
  457.9 6.4 fusion.93
  471.8 11.4 %collective-permute-done.71 = bf16[1280,256]{1,0:T(8,128)(2,1)S(1)} collective-permute-done((bf16[1280,256]{1,0:T(8,128)(2,1)S(1)}, bf16[1280,256]{1,0:T(8,128)(2,1)S(1)}, u32[]{:S(2)}, u32[]{:S(2)}) %collective-permute-start.71) | collective-permute-done | bytes 655392 | tf_op jit(solution)/shard_map/ppermute | solution.py:44
  485.9 4.6 collective-permute-start.75
  493.4 7.6 %collective-permute-done.74 = bf16[1280,256]{1,0:T(8,128)(2,1)S(1)} collective-permute-done((bf16[1280,256]{1,0:T(8,128)(2,1)S(1)}, bf16[1280,256]{1,0:T(8,128)(2,1)S(1)}, u32[]{:S(2)}, u32[]{:S(2)}) %collective-permute-start.74) | collective-permute-done | bytes 655392 | tf_op jit(solution)/shard_map/ppermute | solution.py:43
  501.0 4.6 collective-permute-done.75
  523.9 8.0 %fusion.129 = (f32[1280,2048]{1,0:T(8,128)}, f32[1280,2048]{1,0:T(8,128)S(1)}, f32[1280,256]{1,0:T(8,128)}) fusion(f32[1280,2048]{1,0:T(8,128)} %get-tuple-element.297, f32[1280,2048]{1,0:T(8,128)} %param.7, f32[1280,2048]{1,0:T(8,128)S(1)} %get-tuple-element.298, f32[1280,2048]{1,0:T(8,128)} %param.6, bf16[5120,1280]{1,0:T(8,128)(2,1)S(1)} %bitcast.17, ...), kind=kOutput, calls=%fused_computation.234 | convolution fusion | flops 3368222720 | bytes 22282240 | tf_op jit(solution)/shard_map/dot_general | solution.py:66
  531.9 9.4 %fusion.94 = f32[5120,256]{1,0:T(8,128)S(1)} fusion(bf16[5120,1280]{1,0:T(8,128)(2,1)S(1)} %bitcast.17, f32[1280,256]{1,0:T(8,128)} %get-tuple-element.314, f32[1280,2048]{1,0:T(8,128)} %param.6, f32[1280,2048]{1,0:T(8,128)} %param.7), kind=kOutput, calls=%fused_computation.176 | convolution fusion | flops 3359375360 | bytes 22282240 | tf_op jit(solution)/shard_map/dot_general | solution.py:72
  549.9 8.2 %collective-permute-done.83 = bf16[1280,256]{1,0:T(8,128)(2,1)S(1)} collective-permute-done((bf16[1280,256]{1,0:T(8,128)(2,1)S(1)}, bf16[1280,256]{1,0:T(8,128)(2,1)S(1)}, u32[]{:S(2)}, u32[]{:S(2)}) %collective-permute-start.83) | collective-permute-done | bytes 655392 | tf_op jit(solution)/shard_map/ppermute | solution.py:44
  576.2 4.8 collective-permute-done.86
  590.3 6.1 collective-permute-start.89
  596.3 8.4 %fusion.128 = (f32[1280,2048]{1,0:T(8,128)}, f32[1280,2048]{1,0:T(8,128)}, f32[1280,256]{1,0:T(8,128)}) fusion(f32[1280,2048]{1,0:T(8,128)} %get-tuple-element.295, f32[1280,2048]{1,0:T(8,128)} %param.7, f32[1280,2048]{1,0:T(8,128)} %copy-done.1, f32[1280,2048]{1,0:T(8,128)} %param.6, bf16[5120,1280]{1,0:T(8,128)(2,1)S(1)} %bitcast.17, ...), kind=kOutput, calls=%fused_computation.233 | convolution fusion | flops 3368222720 | bytes 22282240 | tf_op jit(solution)/shard_map/dot_general | solution.py:66
  604.8 6.4 fusion.95
  617.2 10.8 %collective-permute-done.91 = bf16[1280,256]{1,0:T(8,128)(2,1)S(1)} collective-permute-done((bf16[1280,256]{1,0:T(8,128)(2,1)S(1)}, bf16[1280,256]{1,0:T(8,128)(2,1)S(1)}, u32[]{:S(2)}, u32[]{:S(2)}) %collective-permute-start.91) | collective-permute-done | bytes 655392 | tf_op jit(solution)/shard_map/ppermute | solution.py:44
  629.6 6.5 collective-permute-start.93
  (272 shorter events, 299.5 us)
Async XLA Ops:
  7.4 18.4 %collective-permute-start.1 = (bf16[1280,256]{1,0:T(8,128)(2,1)S(1)}, bf16[1280,256]{1,0:T(8,128)(2,1)S(1)}, u32[]{:S(2)}, u32[]{:S(2)}) collective-permute-start(bf16[1280,256]{1,0:T(8,128)(2,1)S(1)} %get-tuple-element.256), channel_id=1, source_target_pairs={{8,0},{16,8},{24,16},{9,1},{17,9},{25,17},{10,2},{18,10},{26,18},{... | collective-permute-start | bytes 1966088 | tf_op jit(solution)/shard_map/ppermute | solution.py:40
  9.8 18.2 %collective-permute-start = (bf16[1280,256]{1,0:T(8,128)(2,1)S(1)}, bf16[1280,256]{1,0:T(8,128)(2,1)}, u32[]{:S(2)}, u32[]{:S(2)}) collective-permute-start(bf16[1280,256]{1,0:T(8,128)(2,1)S(1)} %get-tuple-element.256), channel_id=1, source_target_pairs={{0,8},{8,16},{16,24},{1,9},{9,17},{17,25},{2,10},{10,18},{18,26},{... | collective-permute-start | bytes 1966088 | tf_op jit(solution)/shard_map/ppermute | solution.py:39
  30.3 17.1 %collective-permute-start.2 = (bf16[1280,256]{1,0:T(8,128)(2,1)}, bf16[1280,256]{1,0:T(8,128)(2,1)S(1)}, u32[]{:S(2)}, u32[]{:S(2)}) collective-permute-start(bf16[1280,256]{1,0:T(8,128)(2,1)} %collective-permute-done), channel_id=1, source_target_pairs={{8,16},{16,24},{9,17},{17,25},{10,18},{18,26},{11,19},{19,27},{12,... | collective-permute-start | bytes 1966088 | tf_op jit(solution)/shard_map/ppermute | solution.py:39
  47.4 19.9 %collective-permute-start.4 = (bf16[1280,256]{1,0:T(8,128)(2,1)S(1)}, bf16[1280,256]{1,0:T(8,128)(2,1)}, u32[]{:S(2)}, u32[]{:S(2)}) collective-permute-start(bf16[1280,256]{1,0:T(8,128)(2,1)S(1)} %collective-permute-done.2), channel_id=1, source_target_pairs={{16,24},{17,25},{18,26},{19,27},{20,28},{21,29},{22,30},{23,31}} | collective-permute-start | bytes 1966088 | tf_op jit(solution)/shard_map/ppermute | solution.py:39
  67.4 21.4 %collective-permute-start.7 = (bf16[1280,256]{1,0:T(8,128)(2,1)S(1)}, bf16[1280,256]{1,0:T(8,128)(2,1)S(1)}, u32[]{:S(2)}, u32[]{:S(2)}) collective-permute-start(bf16[1280,256]{1,0:T(8,128)(2,1)S(1)} %get-tuple-element.126), channel_id=1, source_target_pairs={{8,0},{16,8},{24,16},{9,1},{17,9},{25,17},{10,2},{18,10},{26,18},{... | collective-permute-start | bytes 1966088 | tf_op jit(solution)/shard_map/ppermute | solution.py:40
  69.3 19.4 %collective-permute-start.6 = (bf16[1280,256]{1,0:T(8,128)(2,1)S(1)}, bf16[1280,256]{1,0:T(8,128)(2,1)S(1)}, u32[]{:S(2)}, u32[]{:S(2)}) collective-permute-start(bf16[1280,256]{1,0:T(8,128)(2,1)S(1)} %get-tuple-element.126), channel_id=1, source_target_pairs={{0,8},{8,16},{16,24},{1,9},{9,17},{17,25},{2,10},{10,18},{18,26},{... | collective-permute-start | bytes 1966088 | tf_op jit(solution)/shard_map/ppermute | solution.py:39
  133.0 29.8 %collective-permute-start.17 = (bf16[1280,256]{1,0:T(8,128)(2,1)}, bf16[1280,256]{1,0:T(8,128)(2,1)}, u32[]{:S(2)}, u32[]{:S(2)}) collective-permute-start(bf16[1280,256]{1,0:T(8,128)(2,1)} %get-tuple-element.137), channel_id=1, source_target_pairs={{8,0},{16,8},{24,16},{9,1},{17,9},{25,17},{10,2},{18,10},{26,18},{... | collective-permute-start | bytes 1966088 | tf_op jit(solution)/shard_map/ppermute | solution.py:40
  135.1 27.7 %collective-permute-start.16 = (bf16[1280,256]{1,0:T(8,128)(2,1)}, bf16[1280,256]{1,0:T(8,128)(2,1)}, u32[]{:S(2)}, u32[]{:S(2)}) collective-permute-start(bf16[1280,256]{1,0:T(8,128)(2,1)} %get-tuple-element.137), channel_id=1, source_target_pairs={{0,8},{8,16},{16,24},{1,9},{9,17},{17,25},{2,10},{10,18},{18,26},{... | collective-permute-start | bytes 1966088 | tf_op jit(solution)/shard_map/ppermute | solution.py:39
  141.6 21.2 %collective-permute-start.18 = (bf16[1280,256]{1,0:T(8,128)(2,1)}, bf16[1280,256]{1,0:T(8,128)(2,1)}, u32[]{:S(2)}, u32[]{:S(2)}) collective-permute-start(bf16[1280,256]{1,0:T(8,128)(2,1)} %get-tuple-element.138), channel_id=1, source_target_pairs={{0,8},{8,16},{16,24},{1,9},{9,17},{17,25},{2,10},{10,18},{18,26},{... | collective-permute-start | bytes 1966088 | tf_op jit(solution)/shard_map/ppermute | solution.py:43
  143.5 19.3 %collective-permute-start.19 = (bf16[1280,256]{1,0:T(8,128)(2,1)}, bf16[1280,256]{1,0:T(8,128)(2,1)}, u32[]{:S(2)}, u32[]{:S(2)}) collective-permute-start(bf16[1280,256]{1,0:T(8,128)(2,1)} %get-tuple-element.139), channel_id=1, source_target_pairs={{8,0},{16,8},{24,16},{9,1},{17,9},{25,17},{10,2},{18,10},{26,18},{... | collective-permute-start | bytes 1966088 | tf_op jit(solution)/shard_map/ppermute | solution.py:44
  170.7 18.5 %collective-permute-start.20 = (bf16[1280,256]{1,0:T(8,128)(2,1)}, bf16[1280,256]{1,0:T(8,128)(2,1)S(1)}, u32[]{:S(2)}, u32[]{:S(2)}) collective-permute-start(bf16[1280,256]{1,0:T(8,128)(2,1)} %collective-permute-done.16), channel_id=1, source_target_pairs={{8,16},{16,24},{9,17},{17,25},{10,18},{18,26},{11,19},{19,27},{12,... | collective-permute-start | bytes 1966088 | tf_op jit(solution)/shard_map/ppermute | solution.py:39
  190.5 19.1 %collective-permute-start.27 = (bf16[1280,256]{1,0:T(8,128)(2,1)S(1)}, bf16[1280,256]{1,0:T(8,128)(2,1)S(1)}, u32[]{:S(2)}, u32[]{:S(2)}) collective-permute-start(bf16[1280,256]{1,0:T(8,128)(2,1)S(1)} %get-tuple-element.147), channel_id=1, source_target_pairs={{16,8},{24,16},{17,9},{25,17},{18,10},{26,18},{19,11},{27,19},{20,... | collective-permute-start | bytes 1966088 | tf_op jit(solution)/shard_map/ppermute | solution.py:44
  211.1 31.6 %collective-permute-start.29 = (bf16[1280,256]{1,0:T(8,128)(2,1)}, bf16[1280,256]{1,0:T(8,128)(2,1)}, u32[]{:S(2)}, u32[]{:S(2)}) collective-permute-start(bf16[1280,256]{1,0:T(8,128)(2,1)} %get-tuple-element.150), channel_id=1, source_target_pairs={{8,0},{16,8},{24,16},{9,1},{17,9},{25,17},{10,2},{18,10},{26,18},{... | collective-permute-start | bytes 1966088 | tf_op jit(solution)/shard_map/ppermute | solution.py:40
  214.5 28.3 %collective-permute-start.28 = (bf16[1280,256]{1,0:T(8,128)(2,1)}, bf16[1280,256]{1,0:T(8,128)(2,1)}, u32[]{:S(2)}, u32[]{:S(2)}) collective-permute-start(bf16[1280,256]{1,0:T(8,128)(2,1)} %get-tuple-element.150), channel_id=1, source_target_pairs={{0,8},{8,16},{16,24},{1,9},{9,17},{17,25},{2,10},{10,18},{18,26},{... | collective-permute-start | bytes 1966088 | tf_op jit(solution)/shard_map/ppermute | solution.py:39
  222.0 20.8 %collective-permute-start.30 = (bf16[1280,256]{1,0:T(8,128)(2,1)}, bf16[1280,256]{1,0:T(8,128)(2,1)}, u32[]{:S(2)}, u32[]{:S(2)}) collective-permute-start(bf16[1280,256]{1,0:T(8,128)(2,1)} %get-tuple-element.151), channel_id=1, source_target_pairs={{0,8},{8,16},{16,24},{1,9},{9,17},{17,25},{2,10},{10,18},{18,26},{... | collective-permute-start | bytes 1966088 | tf_op jit(solution)/shard_map/ppermute | solution.py:43
  223.9 18.9 %collective-permute-start.31 = (bf16[1280,256]{1,0:T(8,128)(2,1)}, bf16[1280,256]{1,0:T(8,128)(2,1)}, u32[]{:S(2)}, u32[]{:S(2)}) collective-permute-start(bf16[1280,256]{1,0:T(8,128)(2,1)} %get-tuple-element.152), channel_id=1, source_target_pairs={{8,0},{16,8},{24,16},{9,1},{17,9},{25,17},{10,2},{18,10},{26,18},{... | collective-permute-start | bytes 1966088 | tf_op jit(solution)/shard_map/ppermute | solution.py:44
  243.5 18.1 %collective-permute-start.35 = (bf16[1280,256]{1,0:T(8,128)(2,1)S(1)}, bf16[1280,256]{1,0:T(8,128)(2,1)S(1)}, u32[]{:S(2)}, u32[]{:S(2)}) collective-permute-start(bf16[1280,256]{1,0:T(8,128)(2,1)S(1)} %get-tuple-element.156), channel_id=1, source_target_pairs={{24,16},{25,17},{26,18},{27,19},{28,20},{29,21},{30,22},{31,23}} | collective-permute-start | bytes 1966088 | tf_op jit(solution)/shard_map/ppermute | solution.py:44
  244.8 17.1 %collective-permute-start.33 = (bf16[1280,256]{1,0:T(8,128)(2,1)}, bf16[1280,256]{1,0:T(8,128)(2,1)S(1)}, u32[]{:S(2)}, u32[]{:S(2)}) collective-permute-start(bf16[1280,256]{1,0:T(8,128)(2,1)} %collective-permute-done.29), channel_id=1, source_target_pairs={{8,0},{16,8},{9,1},{17,9},{10,2},{18,10},{11,3},{19,11},{12,4},{20... | collective-permute-start | bytes 1966088 | tf_op jit(solution)/shard_map/ppermute | solution.py:40
  262.9 17.9 %collective-permute-start.38 = (bf16[1280,256]{1,0:T(8,128)(2,1)S(1)}, bf16[1280,256]{1,0:T(8,128)(2,1)S(1)}, u32[]{:S(2)}, u32[]{:S(2)}) collective-permute-start(bf16[1280,256]{1,0:T(8,128)(2,1)S(1)} %get-tuple-element.159), channel_id=1, source_target_pairs={{0,8},{8,16},{1,9},{9,17},{2,10},{10,18},{3,11},{11,19},{4,12},{12... | collective-permute-start | bytes 1966088 | tf_op jit(solution)/shard_map/ppermute | solution.py:43
  264.1 18.0 %collective-permute-start.39 = (bf16[1280,256]{1,0:T(8,128)(2,1)S(1)}, bf16[1280,256]{1,0:T(8,128)(2,1)S(1)}, u32[]{:S(2)}, u32[]{:S(2)}) collective-permute-start(bf16[1280,256]{1,0:T(8,128)(2,1)S(1)} %get-tuple-element.160), channel_id=1, source_target_pairs={{16,8},{24,16},{17,9},{25,17},{18,10},{26,18},{19,11},{27,19},{20,... | collective-permute-start | bytes 1966088 | tf_op jit(solution)/shard_map/ppermute | solution.py:44
  285.2 31.5 %collective-permute-start.41 = (bf16[1280,256]{1,0:T(8,128)(2,1)}, bf16[1280,256]{1,0:T(8,128)(2,1)}, u32[]{:S(2)}, u32[]{:S(2)}) collective-permute-start(bf16[1280,256]{1,0:T(8,128)(2,1)} %get-tuple-element.163), channel_id=1, source_target_pairs={{8,0},{16,8},{24,16},{9,1},{17,9},{25,17},{10,2},{18,10},{26,18},{... | collective-permute-start | bytes 1966088 | tf_op jit(solution)/shard_map/ppermute | solution.py:40
  287.5 29.2 %collective-permute-start.40 = (bf16[1280,256]{1,0:T(8,128)(2,1)}, bf16[1280,256]{1,0:T(8,128)(2,1)}, u32[]{:S(2)}, u32[]{:S(2)}) collective-permute-start(bf16[1280,256]{1,0:T(8,128)(2,1)} %get-tuple-element.163), channel_id=1, source_target_pairs={{0,8},{8,16},{16,24},{1,9},{9,17},{17,25},{2,10},{10,18},{18,26},{... | collective-permute-start | bytes 1966088 | tf_op jit(solution)/shard_map/ppermute | solution.py:39
  296.0 20.7 %collective-permute-start.42 = (bf16[1280,256]{1,0:T(8,128)(2,1)}, bf16[1280,256]{1,0:T(8,128)(2,1)}, u32[]{:S(2)}, u32[]{:S(2)}) collective-permute-start(bf16[1280,256]{1,0:T(8,128)(2,1)} %get-tuple-element.164), channel_id=1, source_target_pairs={{0,8},{8,16},{16,24},{1,9},{9,17},{17,25},{2,10},{10,18},{18,26},{... | collective-permute-start | bytes 1966088 | tf_op jit(solution)/shard_map/ppermute | solution.py:43
  297.9 18.7 %collective-permute-start.43 = (bf16[1280,256]{1,0:T(8,128)(2,1)}, bf16[1280,256]{1,0:T(8,128)(2,1)}, u32[]{:S(2)}, u32[]{:S(2)}) collective-permute-start(bf16[1280,256]{1,0:T(8,128)(2,1)} %get-tuple-element.165), channel_id=1, source_target_pairs={{8,0},{16,8},{24,16},{9,1},{17,9},{25,17},{10,2},{18,10},{26,18},{... | collective-permute-start | bytes 1966088 | tf_op jit(solution)/shard_map/ppermute | solution.py:44
  317.4 17.9 %collective-permute-start.47 = (bf16[1280,256]{1,0:T(8,128)(2,1)S(1)}, bf16[1280,256]{1,0:T(8,128)(2,1)S(1)}, u32[]{:S(2)}, u32[]{:S(2)}) collective-permute-start(bf16[1280,256]{1,0:T(8,128)(2,1)S(1)} %get-tuple-element.169), channel_id=1, source_target_pairs={{24,16},{25,17},{26,18},{27,19},{28,20},{29,21},{30,22},{31,23}} | collective-permute-start | bytes 1966088 | tf_op jit(solution)/shard_map/ppermute | solution.py:44
  338.0 19.2 %collective-permute-start.51 = (bf16[1280,256]{1,0:T(8,128)(2,1)S(1)}, bf16[1280,256]{1,0:T(8,128)(2,1)S(1)}, u32[]{:S(2)}, u32[]{:S(2)}) collective-permute-start(bf16[1280,256]{1,0:T(8,128)(2,1)S(1)} %get-tuple-element.173), channel_id=1, source_target_pairs={{16,8},{24,16},{17,9},{25,17},{18,10},{26,18},{19,11},{27,19},{20,... | collective-permute-start | bytes 1966088 | tf_op jit(solution)/shard_map/ppermute | solution.py:44
  359.0 31.6 %collective-permute-start.53 = (bf16[1280,256]{1,0:T(8,128)(2,1)}, bf16[1280,256]{1,0:T(8,128)(2,1)}, u32[]{:S(2)}, u32[]{:S(2)}) collective-permute-start(bf16[1280,256]{1,0:T(8,128)(2,1)} %get-tuple-element.176), channel_id=1, source_target_pairs={{8,0},{16,8},{24,16},{9,1},{17,9},{25,17},{10,2},{18,10},{26,18},{... | collective-permute-start | bytes 1966088 | tf_op jit(solution)/shard_map/ppermute | solution.py:40
  363.0 27.7 %collective-permute-start.52 = (bf16[1280,256]{1,0:T(8,128)(2,1)}, bf16[1280,256]{1,0:T(8,128)(2,1)}, u32[]{:S(2)}, u32[]{:S(2)}) collective-permute-start(bf16[1280,256]{1,0:T(8,128)(2,1)} %get-tuple-element.176), channel_id=1, source_target_pairs={{0,8},{8,16},{16,24},{1,9},{9,17},{17,25},{2,10},{10,18},{18,26},{... | collective-permute-start | bytes 1966088 | tf_op jit(solution)/shard_map/ppermute | solution.py:39
  369.8 20.8 %collective-permute-start.54 = (bf16[1280,256]{1,0:T(8,128)(2,1)}, bf16[1280,256]{1,0:T(8,128)(2,1)}, u32[]{:S(2)}, u32[]{:S(2)}) collective-permute-start(bf16[1280,256]{1,0:T(8,128)(2,1)} %get-tuple-element.177), channel_id=1, source_target_pairs={{0,8},{8,16},{16,24},{1,9},{9,17},{17,25},{2,10},{10,18},{18,26},{... | collective-permute-start | bytes 1966088 | tf_op jit(solution)/shard_map/ppermute | solution.py:43
  371.7 18.9 %collective-permute-start.55 = (bf16[1280,256]{1,0:T(8,128)(2,1)}, bf16[1280,256]{1,0:T(8,128)(2,1)}, u32[]{:S(2)}, u32[]{:S(2)}) collective-permute-start(bf16[1280,256]{1,0:T(8,128)(2,1)} %get-tuple-element.178), channel_id=1, source_target_pairs={{8,0},{16,8},{24,16},{9,1},{17,9},{25,17},{10,2},{18,10},{26,18},{... | collective-permute-start | bytes 1966088 | tf_op jit(solution)/shard_map/ppermute | solution.py:44
  391.4 18.0 %collective-permute-start.59 = (bf16[1280,256]{1,0:T(8,128)(2,1)S(1)}, bf16[1280,256]{1,0:T(8,128)(2,1)S(1)}, u32[]{:S(2)}, u32[]{:S(2)}) collective-permute-start(bf16[1280,256]{1,0:T(8,128)(2,1)S(1)} %get-tuple-element.182), channel_id=1, source_target_pairs={{24,16},{25,17},{26,18},{27,19},{28,20},{29,21},{30,22},{31,23}} | collective-permute-start | bytes 1966088 | tf_op jit(solution)/shard_map/ppermute | solution.py:44
  410.7 18.7 %collective-permute-start.62 = (bf16[1280,256]{1,0:T(8,128)(2,1)S(1)}, bf16[1280,256]{1,0:T(8,128)(2,1)S(1)}, u32[]{:S(2)}, u32[]{:S(2)}) collective-permute-start(bf16[1280,256]{1,0:T(8,128)(2,1)S(1)} %get-tuple-element.185), channel_id=1, source_target_pairs={{0,8},{8,16},{1,9},{9,17},{2,10},{10,18},{3,11},{11,19},{4,12},{12... | collective-permute-start | bytes 1966088 | tf_op jit(solution)/shard_map/ppermute | solution.py:43
  412.0 18.1 %collective-permute-start.63 = (bf16[1280,256]{1,0:T(8,128)(2,1)S(1)}, bf16[1280,256]{1,0:T(8,128)(2,1)S(1)}, u32[]{:S(2)}, u32[]{:S(2)}) collective-permute-start(bf16[1280,256]{1,0:T(8,128)(2,1)S(1)} %get-tuple-element.186), channel_id=1, source_target_pairs={{16,8},{24,16},{17,9},{25,17},{18,10},{26,18},{19,11},{27,19},{20,... | collective-permute-start | bytes 1966088 | tf_op jit(solution)/shard_map/ppermute | solution.py:44
  433.1 31.4 %collective-permute-start.65 = (bf16[1280,256]{1,0:T(8,128)(2,1)}, bf16[1280,256]{1,0:T(8,128)(2,1)}, u32[]{:S(2)}, u32[]{:S(2)}) collective-permute-start(bf16[1280,256]{1,0:T(8,128)(2,1)} %get-tuple-element.189), channel_id=1, source_target_pairs={{8,0},{16,8},{24,16},{9,1},{17,9},{25,17},{10,2},{18,10},{26,18},{... | collective-permute-start | bytes 1966088 | tf_op jit(solution)/shard_map/ppermute | solution.py:40
  435.0 29.5 %collective-permute-start.64 = (bf16[1280,256]{1,0:T(8,128)(2,1)}, bf16[1280,256]{1,0:T(8,128)(2,1)}, u32[]{:S(2)}, u32[]{:S(2)}) collective-permute-start(bf16[1280,256]{1,0:T(8,128)(2,1)} %get-tuple-element.189), channel_id=1, source_target_pairs={{0,8},{8,16},{16,24},{1,9},{9,17},{17,25},{2,10},{10,18},{18,26},{... | collective-permute-start | bytes 1966088 | tf_op jit(solution)/shard_map/ppermute | solution.py:39
  443.8 20.6 %collective-permute-start.66 = (bf16[1280,256]{1,0:T(8,128)(2,1)}, bf16[1280,256]{1,0:T(8,128)(2,1)}, u32[]{:S(2)}, u32[]{:S(2)}) collective-permute-start(bf16[1280,256]{1,0:T(8,128)(2,1)} %get-tuple-element.190), channel_id=1, source_target_pairs={{0,8},{8,16},{16,24},{1,9},{9,17},{17,25},{2,10},{10,18},{18,26},{... | collective-permute-start | bytes 1966088 | tf_op jit(solution)/shard_map/ppermute | solution.py:43
  445.7 18.7 %collective-permute-start.67 = (bf16[1280,256]{1,0:T(8,128)(2,1)}, bf16[1280,256]{1,0:T(8,128)(2,1)}, u32[]{:S(2)}, u32[]{:S(2)}) collective-permute-start(bf16[1280,256]{1,0:T(8,128)(2,1)} %get-tuple-element.191), channel_id=1, source_target_pairs={{8,0},{16,8},{24,16},{9,1},{17,9},{25,17},{10,2},{18,10},{26,18},{... | collective-permute-start | bytes 1966088 | tf_op jit(solution)/shard_map/ppermute | solution.py:44
  465.2 18.1 %collective-permute-start.71 = (bf16[1280,256]{1,0:T(8,128)(2,1)S(1)}, bf16[1280,256]{1,0:T(8,128)(2,1)S(1)}, u32[]{:S(2)}, u32[]{:S(2)}) collective-permute-start(bf16[1280,256]{1,0:T(8,128)(2,1)S(1)} %get-tuple-element.195), channel_id=1, source_target_pairs={{24,16},{25,17},{26,18},{27,19},{28,20},{29,21},{30,22},{31,23}} | collective-permute-start | bytes 1966088 | tf_op jit(solution)/shard_map/ppermute | solution.py:44
  466.5 17.1 %collective-permute-start.69 = (bf16[1280,256]{1,0:T(8,128)(2,1)}, bf16[1280,256]{1,0:T(8,128)(2,1)S(1)}, u32[]{:S(2)}, u32[]{:S(2)}) collective-permute-start(bf16[1280,256]{1,0:T(8,128)(2,1)} %collective-permute-done.65), channel_id=1, source_target_pairs={{8,0},{16,8},{9,1},{17,9},{10,2},{18,10},{11,3},{19,11},{12,4},{20... | collective-permute-start | bytes 1966088 | tf_op jit(solution)/shard_map/ppermute | solution.py:40
  485.9 19.7 %collective-permute-start.75 = (bf16[1280,256]{1,0:T(8,128)(2,1)S(1)}, bf16[1280,256]{1,0:T(8,128)(2,1)S(1)}, u32[]{:S(2)}, u32[]{:S(2)}) collective-permute-start(bf16[1280,256]{1,0:T(8,128)(2,1)S(1)} %get-tuple-element.199), channel_id=1, source_target_pairs={{16,8},{24,16},{17,9},{25,17},{18,10},{26,18},{19,11},{27,19},{20,... | collective-permute-start | bytes 1966088 | tf_op jit(solution)/shard_map/ppermute | solution.py:44
  507.1 34.4 %collective-permute-start.77 = (bf16[1280,256]{1,0:T(8,128)(2,1)}, bf16[1280,256]{1,0:T(8,128)(2,1)}, u32[]{:S(2)}, u32[]{:S(2)}) collective-permute-start(bf16[1280,256]{1,0:T(8,128)(2,1)} %get-tuple-element.202), channel_id=1, source_target_pairs={{8,0},{16,8},{24,16},{9,1},{17,9},{25,17},{10,2},{18,10},{26,18},{... | collective-permute-start | bytes 1966088 | tf_op jit(solution)/shard_map/ppermute | solution.py:40
  511.5 30.0 %collective-permute-start.76 = (bf16[1280,256]{1,0:T(8,128)(2,1)}, bf16[1280,256]{1,0:T(8,128)(2,1)}, u32[]{:S(2)}, u32[]{:S(2)}) collective-permute-start(bf16[1280,256]{1,0:T(8,128)(2,1)} %get-tuple-element.202), channel_id=1, source_target_pairs={{0,8},{8,16},{16,24},{1,9},{9,17},{17,25},{2,10},{10,18},{18,26},{... | collective-permute-start | bytes 1966088 | tf_op jit(solution)/shard_map/ppermute | solution.py:39
  517.8 23.6 %collective-permute-start.78 = (bf16[1280,256]{1,0:T(8,128)(2,1)}, bf16[1280,256]{1,0:T(8,128)(2,1)}, u32[]{:S(2)}, u32[]{:S(2)}) collective-permute-start(bf16[1280,256]{1,0:T(8,128)(2,1)} %get-tuple-element.203), channel_id=1, source_target_pairs={{0,8},{8,16},{16,24},{1,9},{9,17},{17,25},{2,10},{10,18},{18,26},{... | collective-permute-start | bytes 1966088 | tf_op jit(solution)/shard_map/ppermute | solution.py:43
  519.7 21.7 %collective-permute-start.79 = (bf16[1280,256]{1,0:T(8,128)(2,1)}, bf16[1280,256]{1,0:T(8,128)(2,1)}, u32[]{:S(2)}, u32[]{:S(2)}) collective-permute-start(bf16[1280,256]{1,0:T(8,128)(2,1)} %get-tuple-element.204), channel_id=1, source_target_pairs={{8,0},{16,8},{24,16},{9,1},{17,9},{25,17},{10,2},{18,10},{26,18},{... | collective-permute-start | bytes 1966088 | tf_op jit(solution)/shard_map/ppermute | solution.py:44
  563.0 17.9 %collective-permute-start.86 = (bf16[1280,256]{1,0:T(8,128)(2,1)}, bf16[1280,256]{1,0:T(8,128)(2,1)S(1)}, u32[]{:S(2)}, u32[]{:S(2)}) collective-permute-start(bf16[1280,256]{1,0:T(8,128)(2,1)} %get-tuple-element.211), channel_id=1, source_target_pairs={{0,8},{8,16},{1,9},{9,17},{2,10},{10,18},{3,11},{11,19},{4,12},{12... | collective-permute-start | bytes 1966088 | tf_op jit(solution)/shard_map/ppermute | solution.py:43
  564.3 18.5 %collective-permute-start.87 = (bf16[1280,256]{1,0:T(8,128)(2,1)}, bf16[1280,256]{1,0:T(8,128)(2,1)S(1)}, u32[]{:S(2)}, u32[]{:S(2)}) collective-permute-start(bf16[1280,256]{1,0:T(8,128)(2,1)} %get-tuple-element.212), channel_id=1, source_target_pairs={{16,8},{24,16},{17,9},{25,17},{18,10},{26,18},{19,11},{27,19},{20,... | collective-permute-start | bytes 1966088 | tf_op jit(solution)/shard_map/ppermute | solution.py:44
  588.3 23.0 %collective-permute-start.88 = (bf16[1280,256]{1,0:T(8,128)(2,1)}, bf16[1280,256]{1,0:T(8,128)(2,1)}, u32[]{:S(2)}, u32[]{:S(2)}) collective-permute-start(bf16[1280,256]{1,0:T(8,128)(2,1)} %get-tuple-element.227), channel_id=1, source_target_pairs={{0,8},{8,16},{16,24},{1,9},{9,17},{17,25},{2,10},{10,18},{18,26},{... | collective-permute-start | bytes 1966088 | tf_op jit(solution)/shard_map/ppermute | solution.py:43
  590.3 21.1 %collective-permute-start.89 = (bf16[1280,256]{1,0:T(8,128)(2,1)}, bf16[1280,256]{1,0:T(8,128)(2,1)}, u32[]{:S(2)}, u32[]{:S(2)}) collective-permute-start(bf16[1280,256]{1,0:T(8,128)(2,1)} %get-tuple-element.228), channel_id=1, source_target_pairs={{8,0},{16,8},{24,16},{9,1},{17,9},{25,17},{10,2},{18,10},{26,18},{... | collective-permute-start | bytes 1966088 | tf_op jit(solution)/shard_map/ppermute | solution.py:44
  (73 other events, 1179.6 us)
